TPU v7x, 32 devices: a whole 2x2x4 slice. The times are simulated.
32 devices in a mesh: rep: 2 (over x), asset: 8 (over z, y), sample: 2 (over core).
Axes of the slice: x: 2, y: 2, z: 4, core: 2. Of those that a mesh axis runs over, the one named last changes fastest.
Arguments:
- samples: float32 [8, 1024, 32768], P(('rep', 'sample'), None, 'asset'), parts along dimension 0, may hold values from -40 to 40, as said below
- start_panel: float32 [32768, 128], P('asset'), may hold values from -6 to 6
Outputs:
- local_panels: float32 [8, 32768, 128], P(('rep', 'sample'), 'asset'), parts along dimension 0
- subspace: float32 [65536, 128], P(('rep', 'asset')), parts along dimension 0
There are 2 independent parts, one for each index of `rep`. A program takes and returns all parts, laid end to end along the dimension named above; an argument that names none is the same for every part. Nothing has to cross between parts.
Inputs may be any that keep to these rules, and one draw needn't show every extreme that they name: `samples`: returns of each asset with an asset-specific volatility.
All inputs are finite; a program needn't handle non-finite values.
Results may differ from a plain program's by a relative error of at most 0.0003.
Values sent between devices are 32-bit elements; how exact they have to be, the bound alone decides.
No kernel may reach another device: no remote copies, remote signals or barrier semaphores. Data moves between devices by JAX's collectives and lax.ppermute only.
A program may use at most 192 MiB of HBM per device.

v0:
```python
import functools

import jax
import jax.numpy as jnp
from jax import lax
from jax.experimental import pallas as pl
from jax.experimental.pallas import tpu as pltpu
from jax.sharding import PartitionSpec as P

LOCAL_ITERS = 2
FINAL_ITERS = 4


HIGH = lax.Precision.HIGHEST
TILE = 8
PANEL = 4
WIDTH = 512
ROWS = 1024
MEGA = 1024 * 1024


def dot_exact(left, right, dims):
    return lax.dot_general(
        left, right, (dims, ((), ())), precision=HIGH, preferred_element_type=jnp.float32
    )


def inverse_factors(matrices):
    size = matrices[0].shape[0]
    blocks = size // TILE
    full = (TILE, size)
    sublane = lax.broadcasted_iota(jnp.int32, full, 0)
    lane = lax.broadcasted_iota(jnp.int32, full, 1)
    left, right = [], []
    for matrix in matrices:
        symmetric = 0.5 * (matrix + matrix.T)
        left.append([symmetric[TILE * i : TILE * (i + 1)] for i in range(blocks)])
        right.append(
            [jnp.where(lane == sublane + TILE * i, 1.0, 0.0) for i in range(blocks)]
        )
    along = lambda block, row: jnp.broadcast_to(block[row : row + 1], full)
    across = lambda block, column: jnp.broadcast_to(block[:, column : column + 1], full)
    for panel in range(0, blocks, PANEL):
        last = panel + PANEL
        for j in range(panel, last):
            for a, b in zip(left, right):
                columns = [across(a[j], TILE * j + k) for k in range(TILE)]
                d = [[along(columns[k], i) for k in range(i + 1)] for i in range(TILE)]
                scale = []
                for k in range(TILE):
                    scale.append(lax.rsqrt(d[k][k]))
                    for i in range(k + 1, TILE):
                        d[i][k] = d[i][k] * scale[k]
                    for i in range(k + 1, TILE):
                        for m in range(k + 1, i + 1):
                            d[i][m] = d[i][m] - d[i][k] * d[m][k]

                def substitute(parts):
                    for k in range(TILE):
                        for m in range(k):
                            parts[k] = parts[k] - d[k][m] * parts[m]
                        parts[k] = parts[k] * scale[k]
                    return parts

                rows_a = substitute([along(a[j], k) for k in range(TILE)])
                rows_b = substitute([along(b[j], k) for k in range(TILE)])
                for i in range(j + 1, last):
                    weights = substitute([across(a[i], TILE * j + k) for k in range(TILE)])
                    for k in range(TILE):
                        a[i] = a[i] - weights[k] * rows_a[k]
                        b[i] = b[i] - weights[k] * rows_b[k]

                def gather(rows):
                    block = rows[0]
                    for k in range(1, TILE):
                        block = jnp.where(sublane == k, rows[k], block)
                    return block

                a[j], b[j] = gather(rows_a), gather(rows_b)
        if last < blocks:
            for a, b in zip(left, right):
                top_a = jnp.concatenate(a[panel:last], axis=0)
                top_b = jnp.concatenate(b[panel:last], axis=0)
                change = dot_exact(
                    top_a[:, TILE * last :],
                    jnp.concatenate([top_a, top_b], axis=1),
                    ((0,), (0,)),
                )
                for i in range(last, blocks):
                    rows = change[TILE * (i - last) : TILE * (i - last + 1)]
                    a[i] = a[i] - rows[:, :size]
                    b[i] = b[i] - rows[:, size:]
    return [jnp.concatenate(b, axis=0) for b in right]


def split(value):
    high = value.astype(jnp.bfloat16)
    return high, (value - high.astype(jnp.float32)).astype(jnp.bfloat16)


def dot_short(left, right, dims=((1,), (0,))):
    return lax.dot_general(left, right, (dims, ((), ())), preferred_element_type=jnp.float32)


def call(body, grid, in_specs, out_specs, out_shape, scratch, flops, read):
    return pl.pallas_call(
        body,
        grid=grid,
        in_specs=in_specs,
        out_specs=out_specs,
        out_shape=out_shape,
        scratch_shapes=scratch,
        compiler_params=pltpu.CompilerParams(vmem_limit_bytes=52 * MEGA),
        cost_estimate=pl.CostEstimate(flops=flops, bytes_accessed=read, transcendentals=0),
    )


TOKEN = pl.BlockSpec(memory_space=pl.ANY)


def project_kernel(x_ref, panel_ref, token_ref, out_ref, high_ref, low_ref, total):
    step = pl.program_id(0)
    size = panel_ref.shape[1]

    @pl.when(step == 0)
    def _():
        total[...] = jnp.zeros_like(total)

    high, low = split(x_ref[0])
    high_ref[...] = high
    low_ref[...] = low
    panel_high, panel_low = split(panel_ref[...])
    sides = jnp.concatenate(
        [
            jnp.concatenate([panel_high, panel_low], axis=1),
            jnp.concatenate([panel_high, jnp.zeros_like(panel_low)], axis=1),
        ],
        axis=0,
    )
    total[...] += dot_short(jnp.concatenate([high, low], axis=1), sides)

    @pl.when(step == pl.num_programs(0) - 1)
    def _():
        out_ref[...] = (total[:, :size] + total[:, size:]).T


def project(samples, group, panel, slices, index, token):
    _, length, rows = samples.shape
    size = panel.shape[1]
    width = min(WIDTH, rows)
    steps = rows // width // slices
    first = steps * index
    halves = jax.ShapeDtypeStruct((length, steps * width), jnp.bfloat16)
    return call(
        project_kernel,
        (steps,),
        [
            pl.BlockSpec((1, length, width), lambda i: (group, 0, first + i)),
            pl.BlockSpec((width, size), lambda i: (first + i, 0)),
            TOKEN,
        ],
        (
            pl.BlockSpec((size, length), lambda i: (0, 0)),
            pl.BlockSpec((length, width), lambda i: (0, i)),
            pl.BlockSpec((length, width), lambda i: (0, i)),
        ),
        (jax.ShapeDtypeStruct((size, length), jnp.float32), halves, halves),
        [pltpu.VMEM((length, 2 * size), jnp.float32)],
        8 * length * steps * width * size,
        8 * length * steps * width,
    )(samples, panel, token)


def expand_part(pair, high, low):
    size = pair.shape[0] // 2
    both = dot_short(pair, high)
    return (both[:size] + both[size:]) + dot_short(pair[:size], low)


def apply_kernel(high_ref, low_ref, scores_ref, token_ref, out_ref, pair, total):
    step = pl.program_id(0)
    size = scores_ref.shape[0]

    @pl.when(step == 0)
    def _():
        pair[...] = jnp.concatenate(split(scores_ref[...]), axis=0)
        total[...] = jnp.zeros_like(total)

    high, low = high_ref[...], low_ref[...]
    top, rest = split(expand_part(pair[...], high, low))
    sides = jnp.concatenate(
        [
            jnp.concatenate([top, rest], axis=0),
            jnp.concatenate([top, jnp.zeros_like(rest)], axis=0),
        ],
        axis=1,
    )
    total[...] += dot_short(jnp.concatenate([high, low], axis=1), sides, ((1,), (1,)))

    @pl.when(step == pl.num_programs(0) - 1)
    def _():
        out_ref[...] = total[:, :size] + total[:, size:]


def apply(halves, scores, token):
    length, rows = halves[0].shape
    size = scores.shape[0]
    width = min(WIDTH, rows)
    block = pl.BlockSpec((length, width), lambda i: (0, i))
    return call(
        apply_kernel,
        (rows // width,),
        [block, block, pl.BlockSpec((size, length), lambda i: (0, 0)), TOKEN],
        pl.BlockSpec((length, size), lambda i: (0, 0)),
        jax.ShapeDtypeStruct((length, size), jnp.float32),
        [
            pltpu.VMEM((2 * size, length), jnp.bfloat16),
            pltpu.VMEM((length, 2 * size), jnp.float32),
        ],
        16 * length * rows * size,
        4 * length * rows,
    )(*halves, scores, token)


def expand_kernel(*refs):
    *halves, scores_ref, token_ref, out_ref, pair = refs
    step = pl.program_id(0)

    @pl.when(step == 0)
    def _():
        pair[...] = jnp.concatenate(split(scores_ref[...]), axis=0)

    slices = len(halves) // 2
    for index in range(slices):

        @pl.when(step // (pl.num_programs(0) // slices) == index)
        def _():
            high, low = halves[2 * index][...], halves[2 * index + 1][...]
            out_ref[...] = expand_part(pair[...], high, low).T


def expand(halves, scores, token):
    slices = len(halves)
    length, held = halves[0][0].shape
    size = scores.shape[0]
    width = min(WIDTH, held)
    steps = held // width
    blocks = [
        pl.BlockSpec(
            (length, width),
            lambda i, index=index: (0, jnp.clip(i - index * steps, 0, steps - 1)),
        )
        for index in range(slices)
        for _ in range(2)
    ]
    return call(
        expand_kernel,
        (steps * slices,),
        [*blocks, pl.BlockSpec((size, length), lambda i: (0, 0)), TOKEN],
        pl.BlockSpec((width, size), lambda i: (i, 0)),
        jax.ShapeDtypeStruct((held * slices, size), jnp.float32),
        [pltpu.VMEM((2 * size, length), jnp.bfloat16)],
        8 * length * held * slices * size,
        4 * length * held * slices,
    )(*[half for pair in halves for half in pair], scores, token)


def normal_kernel(width_all, first_ref, second_ref, token_ref, out_ref):
    gram = dot_exact(first_ref[...], second_ref[...], ((1,), (0,))) * (1.0 / width_all)
    (inverse,) = inverse_factors([gram])
    out_ref[...] = dot_exact(inverse, second_ref[...], ((1,), (1,)))


def normalise(first, second, width_all, token):
    size, length = first.shape
    whole = lambda held: pl.BlockSpec(held.shape, lambda: (0, 0))
    return pl.pallas_call(
        functools.partial(normal_kernel, width_all),
        in_specs=[whole(first), whole(second), TOKEN],
        out_specs=whole(first),
        out_shape=jax.ShapeDtypeStruct((size, length), jnp.float32),
        compiler_params=pltpu.CompilerParams(vmem_limit_bytes=40 * MEGA),
        cost_estimate=pl.CostEstimate(
            flops=6_000_000_000, bytes_accessed=4 * 3 * size * length, transcendentals=0
        ),
    )(first, second, token)


def own_gram_kernel(own0, own1, out_ref):
    @pl.when(pl.program_id(0) == 0)
    def _():
        out_ref[...] = jnp.zeros_like(out_ref)

    size = own0.shape[1]
    first = ((0,), (0,))
    high, low = split(jnp.concatenate([own0[...], own1[...]], axis=1))
    both = dot_short(high, jnp.concatenate([high, low], axis=1), first)
    mixed = both[:, 2 * size :]
    gram = both[:, : 2 * size] + (dot_short(low, low, first) + (mixed + mixed.T))
    out_ref[0] += gram[:size, :size]
    out_ref[1] += gram[:size, size:]
    out_ref[2] += gram[size:, size:]


def cross_gram_kernel(own0, own1, other0, other1, out_ref):
    @pl.when(pl.program_id(0) == 0)
    def _():
        out_ref[...] = jnp.zeros_like(out_ref)

    size = own0.shape[1]
    swapped = lax.rem(lax.axis_index("sample"), 2) == 1
    c, d = other0[...], other1[...]
    pairs = ((own0[...], jnp.where(swapped, d, c)), (own1[...], jnp.where(swapped, c, d)))
    for k, (left, right) in enumerate(pairs):
        both = dot_short(
            jnp.concatenate(split(left), axis=1),
            jnp.concatenate(split(right), axis=1),
            ((0,), (0,)),
        )
        out_ref[k] += (both[:size, :size] + both[size:, size:]) + (
            both[:size, size:] + both[size:, :size]
        )


def partial_grams(body, count, panels):
    rows, size = panels[0].shape
    height = min(ROWS, rows)
    return call(
        body,
        (rows // height,),
        [pl.BlockSpec((height, size), lambda i: (i, 0))] * len(panels),
        pl.BlockSpec((count, size, size), lambda i: (0, 0, 0)),
        jax.ShapeDtypeStruct((count, size, size), jnp.float32),
        [],
        2 * 30 * rows * size * size,
        4 * len(panels) * rows * size,
    )(*panels)


def final_kernel(
    width_all, first, second, start0, start1, inverse_ref, out_ref, gram, matrix, held, product
):
    count, size, _ = inverse_ref.shape
    at = lambda g: slice(g * size, (g + 1) * size)
    places = (
        (first, ((0, 0), (0, 1), (1, 1), (0, 2), (1, 3))),
        (second, ((2, 2), (2, 3), (3, 3), (2, 1), (3, 0))),
    )
    for parts, where in places:
        for k, (g, h) in enumerate(where):
            gram[at(g), at(h)] = parts[k]
            if g != h:
                gram[at(h), at(g)] = parts[k].T
    inverses = inverse_factors(
        [gram[at(g), at(g)] * (1.0 / width_all) for g in range(count)]
    )
    starts = [start0[0], start0[1], start1[0], start1[1]]
    for g in range(count):
        inverse_ref[g] = inverses[g]
        held[at(g), :] = dot_exact(inverses[g] * (1.0 / count), starts[g], ((1,), (0,)))
        gram[at(g), :] = dot_exact(inverses[g], gram[at(g), :], ((1,), (0,)))
    for h in range(count):
        matrix[:, at(h)] = dot_exact(gram[:, at(h)], inverses[h], ((1,), (1,)))
    product[...] = dot_exact(matrix[...], held[...], ((1,), (0,)))

    def step(_, carry):
        small = dot_exact(held[...], product[...], ((0,), (0,))) * (1.0 / width_all)
        following = product[...] * (1.0 / count)
        ahead = dot_exact(matrix[...], following, ((1,), (0,)))
        (inverse,) = inverse_factors([small])
        weights = dot_exact(held[...], inverse, ((1,), (1,)))
        for g in range(count):
            out_ref[g] = weights[at(g)]
        held[...] = dot_exact(following, inverse, ((1,), (1,)))
        product[...] = dot_exact(ahead, inverse, ((1,), (1,)))
        return carry

    lax.fori_loop(0, FINAL_ITERS, step, 0)
    for g in range(count):
        out_ref[g] = dot_exact(inverse_ref[g], out_ref[g], ((0,), (0,)))


def final_iterations(first, second, start0, start1, width_all):
    size = first.shape[-1]
    groups_all = 4
    out = jax.ShapeDtypeStruct((groups_all, size, size), jnp.float32)
    wide = groups_all * size
    return pl.pallas_call(
        functools.partial(final_kernel, width_all),
        out_shape=(out, out),
        scratch_shapes=[
            pltpu.VMEM((wide, wide), jnp.float32),
            pltpu.VMEM((wide, wide), jnp.float32),
            pltpu.VMEM((wide, size), jnp.float32),
            pltpu.VMEM((wide, size), jnp.float32),
        ],
        compiler_params=pltpu.CompilerParams(vmem_limit_bytes=40 * MEGA),
    )(first, second, start0, start1)


def output_kernel(own0, own1, other0, other1, inverse_ref, weight_ref, panel_ref, out_ref, sides):
    size = own0.shape[1]
    core = lax.rem(lax.axis_index("sample"), 2)

    @pl.when(pl.program_id(0) == 0)
    def _():
        def side(value, slot):
            high, low = split(value)
            sides[slot, :size, :size] = high
            sides[slot, :size, size:] = low
            sides[slot, size:, :size] = high
            sides[slot, size:, size:] = jnp.zeros_like(low)

        for g in range(2):
            side(inverse_ref[2 * core + g].T, g)
            side(weight_ref[2 * core + g], 2 + g)
            side(weight_ref[2 * (1 - core) + g], 4 + g)

    def product(halves, slot):
        both = dot_short(halves, sides[slot])
        return both[:, :size] + both[:, size:]

    sums = []
    for k, pair in enumerate(((own0, own1), (other0, other1))):
        parts = []
        for g in range(2):
            halves = jnp.concatenate(split(pair[g][...]), axis=1)
            if k == 0:
                panel_ref[g] = product(halves, g)
            parts.append(product(halves, 2 * (k + 1) + g))
        sums.append(parts[0] + parts[1])
    out_ref[...] = sums[0] + sums[1]


def outputs(own, other, inverses, weights):
    rows, size = own[0].shape
    height = min(ROWS, rows)
    whole = pl.BlockSpec(inverses.shape, lambda i: (0, 0, 0))
    return call(
        output_kernel,
        (rows // height,),
        [pl.BlockSpec((height, size), lambda i: (i, 0))] * 4 + [whole, whole],
        (
            pl.BlockSpec((2, height, size), lambda i: (0, i, 0)),
            pl.BlockSpec((height, size), lambda i: (i, 0)),
        ),
        (
            jax.ShapeDtypeStruct((2, rows, size), jnp.float32),
            jax.ShapeDtypeStruct((rows, size), jnp.float32),
        ),
        [pltpu.VMEM((6, 2 * size, 2 * size), jnp.bfloat16)],
        2 * 24 * rows * size * size,
        4 * 7 * rows * size,
    )(*own, *other, inverses, weights)


class Total:
    def __init__(self, value):
        self.count, self.cores = lax.axis_size("asset"), lax.axis_size("sample")
        self.bits = self.count.bit_length() - 1
        self.orders = [list(range(self.bits)), list(range(1, self.bits)) + [0]]
        self.place, self.core = lax.axis_index("asset"), lax.axis_index("sample")
        self.shape = value.shape
        self.held = value.reshape((-1, value.shape[-1]))
        self.round = 0
        self.start()

    @property
    def rounds(self):
        return 2 * self.bits

    def stage(self):
        return min(self.round, self.rounds - 1 - self.round)

    def mine(self):
        stage = self.stage()
        bit = jnp.where(self.core % 2 == 0, self.orders[0][stage], self.orders[1][stage])
        return (self.place >> bit) & 1

    def start(self):
        stage, mine = self.stage(), self.mine()
        if self.round < self.bits:
            halves = self.held.reshape((2, -1, self.shape[-1]))
            self.sent = lax.dynamic_index_in_dim(halves, 1 - mine, 0, keepdims=False)
            self.kept = lax.dynamic_index_in_dim(halves, mine, 0, keepdims=False)
        else:
            self.sent = self.kept = self.held
        pairs = [
            (a * self.cores + c, (a ^ (1 << self.orders[c % 2][stage])) * self.cores + c)
            for a in range(self.count)
            for c in range(self.cores)
        ]
        self.arriving = lax.ppermute(self.sent, ("asset", "sample"), pairs)

    def step(self):
        if self.round < self.bits:
            self.held = self.kept + self.arriving
        else:
            self.held = jnp.where(
                self.mine() == 0,
                jnp.concatenate([self.kept, self.arriving], axis=0),
                jnp.concatenate([self.arriving, self.kept], axis=0),
            )
        self.round += 1
        if self.round < self.rounds:
            self.start()

    def finish(self):
        while self.round < self.rounds:
            self.step()
        return self.held.reshape(self.shape)


def shards(samples, start_panel):
    rows, size = start_panel.shape
    width_all = rows * lax.axis_size("asset")
    core = lax.axis_index("sample")
    swap = lambda held: lax.ppermute(held, "sample", [(0, 1), (1, 0)])
    steps = rows // min(WIDTH, rows)
    slices = next(n for n in (4, 2, 1) if steps % n == 0)

    def beside(result, total):
        if total.round < total.rounds:
            result, total.arriving = lax.optimization_barrier((result, total.arriving))
        return result

    def in_slices(run, total):
        done = []
        for index in range(slices):
            if index and total.round < total.rounds:
                total.step()
            done.append(beside(run(index, total.sent), total))
        return done

    none = jnp.zeros((8, 128), jnp.float32)
    added = lambda values: functools.reduce(jnp.add, values)
    parts0 = [project(samples, 0, start_panel, 2, k, none) for k in range(2)]
    first0 = Total(added([part[0] for part in parts0]))
    parts1 = in_slices(
        lambda k, token: project(samples, 1, start_panel, slices, k, token), first0
    )
    first1 = Total(added([part[0] for part in parts1]))
    while first0.round < first0.rounds:
        first0.step()
        if first1.round < first1.rounds:
            first1.step()
    halves0 = [part[1:] for part in parts0]
    halves1 = [part[1:] for part in parts1]
    scores0 = first0.finish()
    pieces = []
    for k, half in enumerate(halves0):
        pieces.append(beside(apply(half, scores0, first1.sent), first1))
        first1.step() if first1.round < first1.rounds else None
    scores1 = first1.finish()
    second0 = Total(added(pieces))
    second1 = Total(
        added(in_slices(lambda k, token: apply(halves1[k], scores1, token), second0))
    )
    while second0.round < second0.rounds:
        second0.step()
        if second1.round < second1.rounds - 2:
            second1.step()
    normal0 = beside(normalise(scores0, second0.finish(), width_all, second1.sent), second1)
    second1.step()
    own0 = beside(expand(halves0, normal0, second1.sent), second1)
    other0 = swap(own0)
    normal1 = normalise(scores1, second1.finish(), width_all, own0)
    own1 = expand(halves1, normal1, none)
    other1 = swap(own1)
    starts = jnp.einsum(
        "gks,gls->gkl",
        jnp.stack([normal0, normal1]),
        jnp.stack([scores0, scores1]),
        precision=HIGH,
    )
    other_starts = swap(starts)
    grams = jnp.concatenate(
        [
            partial_grams(own_gram_kernel, 3, (own0, own1)),
            partial_grams(cross_gram_kernel, 2, (own0, own1, other0, other1)),
        ]
    )
    grams = Total(grams).finish()
    other_grams = swap(grams)
    ordered = lambda a, b: (jnp.where(core == 0, a, b), jnp.where(core == 0, b, a))
    inverses, weights = final_iterations(
        *ordered(grams, other_grams), *ordered(starts, other_starts), width_all
    )
    return outputs((own0, own1), (other0, other1), inverses, weights)


def solution(mesh):
    placed = (P(("rep", "sample"), None, "asset"), P("asset", None))
    return jax.shard_map(
        shards,
        mesh=mesh,
        in_specs=placed,
        out_specs=(P(("rep", "sample"), "asset", None), P(("rep", "asset"), None)),
        check_vma=False,
    )
```

profile of v0, /device:TPU:0, one launch (start us, length us, event | category | flops | bytes accessed | tf_op | source)
XLA Modules:
  0.0 276.1 jit_solution(11369922149511576113)
XLA Ops:
  0.6 8.6 %shard_map.42 = (f32[128,1024]{1,0:T(8,128)S(1)}, bf16[1024,2048]{1,0:T(8,128)(2,1)}, bf16[1024,2048]{1,0:T(8,128)(2,1)}) custom-call(f32[2,1024,4096]{2,1,0:T(8,128)} %x_ref.11, f32[4096,128]{1,0:T(8,128)} %panel_ref.11, f32[8,128]{1,0:T(8,128)S(1)} %broadcast_in_dim.3.token_ref.refs_9_), custom_call_target="tpu_custom_call" | custom-call | flops 2147483648 | bytes 16777216 | tf_op jit(solution)/shard_map/pallas_call | solution.py:154
  9.2 8.5 %shard_map.41 = (f32[128,1024]{1,0:T(8,128)S(1)}, bf16[1024,2048]{1,0:T(8,128)(2,1)}, bf16[1024,2048]{1,0:T(8,128)(2,1)}) custom-call(f32[2,1024,4096]{2,1,0:T(8,128)} %x_ref.11, f32[4096,128]{1,0:T(8,128)} %panel_ref.11, f32[8,128]{1,0:T(8,128)S(1)} %broadcast_in_dim.3.token_ref.refs_9_), custom_call_target="tpu_custom_call" | custom-call | flops 2147483648 | bytes 16777216 | tf_op jit(solution)/shard_map/pallas_call | solution.py:154
  20.9 4.7 %shard_map.43 = (f32[128,1024]{1,0:T(8,128)S(1)}, bf16[1024,1024]{1,0:T(8,128)(2,1)}, bf16[1024,1024]{1,0:T(8,128)(2,1)}) custom-call(f32[2,1024,4096]{2,1,0:T(8,128)} %x_ref.11, f32[4096,128]{1,0:T(8,128)} %panel_ref.11, f32[64,1024]{1,0:T(8,128)S(1)} %dynamic-slice_bitcast_fusion.3.token_ref), custom_call_target="tpu_custom_call" | custom-call | flops 1073741824 | bytes 8388608 | tf_op jit(solution)/shard_map/pallas_call | solution.py:154
  27.5 4.7 %shard_map.44 = (f32[128,1024]{1,0:T(8,128)S(1)}, bf16[1024,1024]{1,0:T(8,128)(2,1)}, bf16[1024,1024]{1,0:T(8,128)(2,1)}) custom-call(f32[2,1024,4096]{2,1,0:T(8,128)} %x_ref.11, f32[4096,128]{1,0:T(8,128)} %panel_ref.11, f32[32,1024]{1,0:T(8,128)S(1)} %dynamic-slice_bitcast_fusion.8.token_ref), custom_call_target="tpu_custom_call" | custom-call | flops 1073741824 | bytes 8388608 | tf_op jit(solution)/shard_map/pallas_call | solution.py:154
  34.9 4.8 %shard_map.45 = (f32[128,1024]{1,0:T(8,128)S(1)}, bf16[1024,1024]{1,0:T(8,128)(2,1)}, bf16[1024,1024]{1,0:T(8,128)(2,1)}) custom-call(f32[2,1024,4096]{2,1,0:T(8,128)} %x_ref.11, f32[4096,128]{1,0:T(8,128)} %panel_ref.11, f32[16,1024]{1,0:T(8,128)S(1)} %dynamic-slice_bitcast_fusion.13.token_ref), custom_call_target="tpu_custom_call" | custom-call | flops 1073741824 | bytes 8388608 | tf_op jit(solution)/shard_map/pallas_call | solution.py:154
  40.3 4.7 %shard_map.46 = (f32[128,1024]{1,0:T(8,128)S(1)}, bf16[1024,1024]{1,0:T(8,128)(2,1)}, bf16[1024,1024]{1,0:T(8,128)(2,1)}) custom-call(f32[2,1024,4096]{2,1,0:T(8,128)} %x_ref.11, f32[4096,128]{1,0:T(8,128)} %panel_ref.11, f32[16,1024]{1,0:T(8,128)S(1)} %bitcast_add_fusion.13.token_ref), custom_call_target="tpu_custom_call" | custom-call | flops 1073741824 | bytes 8388608 | tf_op jit(solution)/shard_map/pallas_call | solution.py:154
  55.0 4.6 %collective-permute-done.7 = f32[32,1024]{1,0:T(8,128)S(1)} collective-permute-done((f32[32,1024]{1,0:T(8,128)S(1)}, f32[32,1024]{1,0:T(8,128)S(1)}, u32[]{:S(2)}, u32[]{:S(2)}) %collective-permute-start.7) | collective-permute-done | bytes 131104 | tf_op jit(solution)/shard_map/ppermute | solution.py:493
  60.5 4.6 %collective-permute-done.8 = f32[16,1024]{1,0:T(8,128)S(1)} collective-permute-done((f32[16,1024]{1,0:T(8,128)S(1)}, f32[16,1024]{1,0:T(8,128)S(1)}, u32[]{:S(2)}, u32[]{:S(2)}) %collective-permute-start.8) | collective-permute-done | bytes 65568 | tf_op jit(solution)/shard_map/ppermute | solution.py:493
  65.8 7.2 %shard_map.47 = f32[1024,128]{1,0:T(8,128)S(1)} custom-call(bf16[1024,2048]{1,0:T(8,128)(2,1)} %get-tuple-element.54.high_ref.refs_0_, bf16[1024,2048]{1,0:T(8,128)(2,1)} %get-tuple-element.55.low_ref.refs_1_, f32[128,1024]{1,0:T(8,128)S(1)} %maximum_select_fusion.scores_ref.first_ref, f32[16,1024]{1,0:T(8,128)S(1)} %bitcast_add_fusion.12.token_ref), custom_call_target="tpu_custom_call" | custom-call | flops 4294967296 | bytes 8388608 | tf_op jit(solution)/shard_map/pallas_call | solution.py:210
  75.2 7.2 %shard_map.48 = f32[1024,128]{1,0:T(8,128)S(1)} custom-call(bf16[1024,2048]{1,0:T(8,128)(2,1)} %get-tuple-element.56.high_ref.refs_2_, bf16[1024,2048]{1,0:T(8,128)(2,1)} %get-tuple-element.57.low_ref.refs_3_, f32[128,1024]{1,0:T(8,128)S(1)} %maximum_select_fusion.scores_ref.first_ref, f32[32,1024]{1,0:T(8,128)S(1)} %maximum_select_fusion.13.token_ref), custom_call_target="tpu_custom_call" | custom-call | flops 4294967296 | bytes 8388608 | tf_op jit(solution)/shard_map/pallas_call | solution.py:210
  113.8 4.9 %collective-permute-done.18 = f32[512,128]{1,0:T(8,128)S(1)} collective-permute-done((f32[512,128]{1,0:T(8,128)S(1)}, f32[512,128]{1,0:T(8,128)S(1)}, u32[]{:S(2)}, u32[]{:S(2)}) %collective-permute-start.18) | collective-permute-done | bytes 262176 | tf_op jit(solution)/shard_map/ppermute | solution.py:493
  129.7 5.4 %shard_map.53.refs_4_ = f32[128,1024]{1,0:T(8,128)S(1)} custom-call(f32[128,1024]{1,0:T(8,128)S(1)} %maximum_select_fusion.scores_ref.first_ref, f32[1024,128]{1,0:T(8,128)S(1)} %maximum_select_fusion.2.second_ref, f32[128,128]{1,0:T(8,128)S(1)} %bitcast_add_fusion.10.token_ref), custom_call_target="tpu_custom_call" | custom-call | flops 6000000000 | bytes 1572864 | tf_op jit(solution)/shard_map/pallas_call | solution.py:277
  139.1 11.6 %shard_map.54.token_ref.own0 = f32[4096,128]{1,0:T(8,128)} custom-call(bf16[1024,2048]{1,0:T(8,128)(2,1)} %get-tuple-element.54.high_ref.refs_0_, bf16[1024,2048]{1,0:T(8,128)(2,1)} %get-tuple-element.55.low_ref.refs_1_, bf16[1024,2048]{1,0:T(8,128)(2,1)} %get-tuple-element.56.high_ref.refs_2_, bf16[1024,2048]{1,0:T(8,128)(2,1)} %get-tuple-element.57.low_ref.refs_3_, ...), custom_call_target="tpu_custom_call" | custom-call | flops 4294967296 | bytes 16777216 | tf_op jit(solution)/shard_map/pallas_call | solution.py:256
  150.9 6.3 %collective-permute-done.23 = f32[512,128]{1,0:T(8,128)S(1)} collective-permute-done((f32[512,128]{1,0:T(8,128)S(1)}, f32[512,128]{1,0:T(8,128)S(1)}, u32[]{:S(2)}, u32[]{:S(2)}) %collective-permute-start.23) | collective-permute-done | bytes 262176 | tf_op jit(solution)/shard_map/ppermute | solution.py:493
  158.8 5.4 %shard_map.55.refs_8_ = f32[128,1024]{1,0:T(8,128)S(1)} custom-call(f32[128,1024]{1,0:T(8,128)S(1)} %maximum_select_fusion.1.scores_ref.first_ref, f32[1024,128]{1,0:T(8,128)S(1)} %maximum_select_fusion.3.second_ref, f32[4096,128]{1,0:T(8,128)S(1)} %copy-done), custom_call_target="tpu_custom_call" | custom-call | flops 6000000000 | bytes 1572864 | tf_op jit(solution)/shard_map/pallas_call | solution.py:277
  164.3 12.8 %shard_map.56.own1 = f32[4096,128]{1,0:T(8,128)} custom-call(bf16[1024,1024]{1,0:T(8,128)(2,1)} %get-tuple-element.83.high_ref.refs_0_, bf16[1024,1024]{1,0:T(8,128)(2,1)} %get-tuple-element.84.low_ref.refs_1_, bf16[1024,1024]{1,0:T(8,128)(2,1)} %get-tuple-element.87.high_ref.refs_2_, bf16[1024,1024]{1,0:T(8,128)(2,1)} %get-tuple-element.88.low_ref.refs_3_, ...), custom_call_target="tpu_custom_call" | custom-call | flops 4294967296 | bytes 16777216 | tf_op jit(solution)/shard_map/pallas_call | solution.py:256
  184.2 13.6 %shard_map.58 = f32[2,128,128]{2,1,0:T(8,128)S(1)} custom-call(f32[4096,128]{1,0:T(8,128)} %shard_map.54.token_ref.own0, f32[4096,128]{1,0:T(8,128)} %shard_map.56.own1, f32[4096,128]{1,0:T(8,128)} %copy-done.1, f32[4096,128]{1,0:T(8,128)} %copy-done.2), custom_call_target="tpu_custom_call" | custom-call | flops 4026531840 | bytes 8388608 | tf_op jit(solution)/shard_map/pallas_call | solution.py:328
  197.9 5.3 %collective-permute-done.26 = f32[320,128]{1,0:T(8,128)S(1)} collective-permute-done((f32[320,128]{1,0:T(8,128)S(1)}, f32[320,128]{1,0:T(8,128)S(1)}, u32[]{:S(2)}, u32[]{:S(2)}) %collective-permute-start.26) | collective-permute-done | bytes 163872 | tf_op jit(solution)/shard_map/ppermute | solution.py:493
  203.4 5.1 %collective-permute-done.27 = f32[160,128]{1,0:T(8,128)S(1)} collective-permute-done((f32[160,128]{1,0:T(8,128)S(1)}, f32[160,128]{1,0:T(8,128)S(1)}, u32[]{:S(2)}, u32[]{:S(2)}) %collective-permute-start.27) | collective-permute-done | bytes 81952 | tf_op jit(solution)/shard_map/ppermute | solution.py:493
  208.6 4.8 %collective-permute-done.28 = f32[80,128]{1,0:T(8,128)S(1)} collective-permute-done((f32[80,128]{1,0:T(8,128)S(1)}, f32[80,128]{1,0:T(8,128)S(1)}, u32[]{:S(2)}, u32[]{:S(2)}) %collective-permute-start.28) | collective-permute-done | bytes 40992 | tf_op jit(solution)/shard_map/ppermute | solution.py:493
  213.5 5.7 %collective-permute-done.29 = f32[80,128]{1,0:T(8,128)S(1)} collective-permute-done((f32[80,128]{1,0:T(8,128)S(1)}, f32[80,128]{1,0:T(8,128)S(1)}, u32[]{:S(2)}, u32[]{:S(2)}) %collective-permute-start.29) | collective-permute-done | bytes 40992 | tf_op jit(solution)/shard_map/ppermute | solution.py:493
  219.4 5.2 %collective-permute-done.30 = f32[160,128]{1,0:T(8,128)S(1)} collective-permute-done((f32[160,128]{1,0:T(8,128)S(1)}, f32[160,128]{1,0:T(8,128)S(1)}, u32[]{:S(2)}, u32[]{:S(2)}) %collective-permute-start.30) | collective-permute-done | bytes 81952 | tf_op jit(solution)/shard_map/ppermute | solution.py:493
  231.7 35.8 %shard_map.59 = (f32[4,128,128]{2,1,0:T(8,128)S(1)}, f32[4,128,128]{2,1,0:T(8,128)S(1)}) custom-call(f32[5,128,128]{2,1,0:T(8,128)S(1)} %get-tuple-element.107.first, f32[5,128,128]{2,1,0:T(8,128)S(1)} %get-tuple-element.106.second, f32[2,128,128]{2,1,0:T(8,128)S(1)} %get-tuple-element.109.start0, f32[2,128,128]{2,1,0:T(8,128)S(1)} %get-tuple-element.108.start1), custom_call_target="tpu_custom_call" | custom-call | tf_op jit(solution)/shard_map/pallas_call | solution.py:388
  267.6 8.3 %shard_map.60 = (f32[2,4096,128]{2,1,0:T(8,128)}, f32[4096,128]{1,0:T(8,128)}) custom-call(f32[4096,128]{1,0:T(8,128)} %shard_map.54.token_ref.own0, f32[4096,128]{1,0:T(8,128)} %shard_map.56.own1, f32[4096,128]{1,0:T(8,128)} %copy-done.1, f32[4096,128]{1,0:T(8,128)} %copy-done.2, f32[4,128,128]{2,1,0:T(8,128)S(1)} %get-tuple-element.104.inverse_ref, ...), custom_call_target="tpu_custom_call" | custom-call | flops 3221225472 | bytes 14680064 | tf_op jit(solution)/shard_map/pallas_call | solution.py:439
  (126 shorter events, 84.6 us)
Async XLA Ops:
  17.9 7.8 %collective-permute-start = (f32[64,1024]{1,0:T(8,128)S(1)}, f32[64,1024]{1,0:T(8,128)S(1)}, u32[]{:S(2)}, u32[]{:S(2)}) collective-permute-start(f32[64,1024]{1,0:T(8,128)S(1)} %dynamic-slice_bitcast_fusion.3.token_ref), channel_id=1, source_target_pairs={{0,2},{1,5},{2,0},{3,7},{4,6},{5,1},{6,4},{7,3},{8,10},{9,13},{10,... | collective-permute-start | bytes 786440 | tf_op jit(solution)/shard_map/ppermute | solution.py:493
  25.7 6.5 %collective-permute-start.1 = (f32[32,1024]{1,0:T(8,128)S(1)}, f32[32,1024]{1,0:T(8,128)S(1)}, u32[]{:S(2)}, u32[]{:S(2)}) collective-permute-start(f32[32,1024]{1,0:T(8,128)S(1)} %dynamic-slice_bitcast_fusion.8.token_ref), channel_id=1, source_target_pairs={{0,4},{1,9},{2,6},{3,11},{4,0},{5,13},{6,2},{7,15},{8,12},{9,1},{1... | collective-permute-start | bytes 393224 | tf_op jit(solution)/shard_map/ppermute | solution.py:493
  32.3 7.4 %collective-permute-start.2 = (f32[16,1024]{1,0:T(8,128)S(1)}, f32[16,1024]{1,0:T(8,128)S(1)}, u32[]{:S(2)}, u32[]{:S(2)}) collective-permute-start(f32[16,1024]{1,0:T(8,128)S(1)} %dynamic-slice_bitcast_fusion.13.token_ref), channel_id=1, source_target_pairs={{0,8},{1,3},{2,10},{3,1},{4,12},{5,7},{6,14},{7,5},{8,0},{9,11},{1... | collective-permute-start | bytes 196616 | tf_op jit(solution)/shard_map/ppermute | solution.py:493
  39.7 5.9 %collective-permute-start.3 = (f32[16,1024]{1,0:T(8,128)S(1)}, f32[16,1024]{1,0:T(8,128)S(1)}, u32[]{:S(2)}, u32[]{:S(2)}) collective-permute-start(f32[16,1024]{1,0:T(8,128)S(1)} %bitcast_add_fusion.13.token_ref), channel_id=1, source_target_pairs={{0,8},{1,3},{2,10},{3,1},{4,12},{5,7},{6,14},{7,5},{8,0},{9,11},{1... | collective-permute-start | bytes 196616 | tf_op jit(solution)/shard_map/ppermute | solution.py:493
  45.8 6.4 %collective-permute-start.6 = (f32[64,1024]{1,0:T(8,128)S(1)}, f32[64,1024]{1,0:T(8,128)S(1)}, u32[]{:S(2)}, u32[]{:S(2)}) collective-permute-start(f32[64,1024]{1,0:T(8,128)S(1)} %dynamic-slice_bitcast_fusion.2), channel_id=1, source_target_pairs={{0,2},{1,5},{2,0},{3,7},{4,6},{5,1},{6,4},{7,3},{8,10},{9,13},{10,... | collective-permute-start | bytes 786440 | tf_op jit(solution)/shard_map/ppermute | solution.py:493
  47.4 6.0 %collective-permute-start.4 = (f32[32,1024]{1,0:T(8,128)S(1)}, f32[32,1024]{1,0:T(8,128)S(1)}, u32[]{:S(2)}, u32[]{:S(2)}) collective-permute-start(f32[32,1024]{1,0:T(8,128)S(1)} %maximum_select_fusion.12), channel_id=1, source_target_pairs={{0,4},{1,9},{2,6},{3,11},{4,0},{5,13},{6,2},{7,15},{8,12},{9,1},{1... | collective-permute-start | bytes 393224 | tf_op jit(solution)/shard_map/ppermute | solution.py:493
  52.3 7.3 %collective-permute-start.7 = (f32[32,1024]{1,0:T(8,128)S(1)}, f32[32,1024]{1,0:T(8,128)S(1)}, u32[]{:S(2)}, u32[]{:S(2)}) collective-permute-start(f32[32,1024]{1,0:T(8,128)S(1)} %dynamic-slice_bitcast_fusion.7), channel_id=1, source_target_pairs={{0,4},{1,9},{2,6},{3,11},{4,0},{5,13},{6,2},{7,15},{8,12},{9,1},{1... | collective-permute-start | bytes 393224 | tf_op jit(solution)/shard_map/ppermute | solution.py:493
  53.4 7.1 %collective-permute-start.5 = (f32[64,1024]{1,0:T(8,128)S(1)}, f32[64,1024]{1,0:T(8,128)S(1)}, u32[]{:S(2)}, u32[]{:S(2)}) collective-permute-start(f32[64,1024]{1,0:T(8,128)S(1)} %maximum_select_fusion.7), channel_id=1, source_target_pairs={{0,2},{1,5},{2,0},{3,7},{4,6},{5,1},{6,4},{7,3},{8,10},{9,13},{10,... | collective-permute-start | bytes 786440 | tf_op jit(solution)/shard_map/ppermute | solution.py:493
  59.7 5.5 %collective-permute-start.8 = (f32[16,1024]{1,0:T(8,128)S(1)}, f32[16,1024]{1,0:T(8,128)S(1)}, u32[]{:S(2)}, u32[]{:S(2)}) collective-permute-start(f32[16,1024]{1,0:T(8,128)S(1)} %dynamic-slice_bitcast_fusion.12), channel_id=1, source_target_pairs={{0,8},{1,3},{2,10},{3,1},{4,12},{5,7},{6,14},{7,5},{8,0},{9,11},{1... | collective-permute-start | bytes 196616 | tf_op jit(solution)/shard_map/ppermute | solution.py:493
  65.2 7.9 %collective-permute-start.9 = (f32[16,1024]{1,0:T(8,128)S(1)}, f32[16,1024]{1,0:T(8,128)S(1)}, u32[]{:S(2)}, u32[]{:S(2)}) collective-permute-start(f32[16,1024]{1,0:T(8,128)S(1)} %bitcast_add_fusion.12.token_ref), channel_id=1, source_target_pairs={{0,8},{1,3},{2,10},{3,1},{4,12},{5,7},{6,14},{7,5},{8,0},{9,11},{1... | collective-permute-start | bytes 196616 | tf_op jit(solution)/shard_map/ppermute | solution.py:493
  73.1 9.4 %collective-permute-start.10 = (f32[32,1024]{1,0:T(8,128)S(1)}, f32[32,1024]{1,0:T(8,128)S(1)}, u32[]{:S(2)}, u32[]{:S(2)}) collective-permute-start(f32[32,1024]{1,0:T(8,128)S(1)} %maximum_select_fusion.13.token_ref), channel_id=1, source_target_pairs={{0,4},{1,9},{2,6},{3,11},{4,0},{5,13},{6,2},{7,15},{8,12},{9,1},{1... | collective-permute-start | bytes 393224 | tf_op jit(solution)/shard_map/ppermute | solution.py:493
  82.5 6.4 %collective-permute-start.11 = (f32[64,1024]{1,0:T(8,128)S(1)}, f32[64,1024]{1,0:T(8,128)S(1)}, u32[]{:S(2)}, u32[]{:S(2)}) collective-permute-start(f32[64,1024]{1,0:T(8,128)S(1)} %maximum_select_fusion.8), channel_id=1, source_target_pairs={{0,2},{1,5},{2,0},{3,7},{4,6},{5,1},{6,4},{7,3},{8,10},{9,13},{10,... | collective-permute-start | bytes 786440 | tf_op jit(solution)/shard_map/ppermute | solution.py:493
  84.3 9.0 %collective-permute-start.12 = (f32[512,128]{1,0:T(8,128)S(1)}, f32[512,128]{1,0:T(8,128)S(1)}, u32[]{:S(2)}, u32[]{:S(2)}) collective-permute-start(f32[512,128]{1,0:T(8,128)S(1)} %dynamic-slice_bitcast_fusion.1.token_ref), channel_id=1, source_target_pairs={{0,2},{1,5},{2,0},{3,7},{4,6},{5,1},{6,4},{7,3},{8,10},{9,13},{10,... | collective-permute-start | bytes 786440 | tf_op jit(solution)/shard_map/ppermute | solution.py:493
  98.5 6.3 %collective-permute-start.14 = (f32[128,128]{1,0:T(8,128)S(1)}, f32[128,128]{1,0:T(8,128)S(1)}, u32[]{:S(2)}, u32[]{:S(2)}) collective-permute-start(f32[128,128]{1,0:T(8,128)S(1)} %dynamic-slice_bitcast_fusion.11.token_ref), channel_id=1, source_target_pairs={{0,8},{1,3},{2,10},{3,1},{4,12},{5,7},{6,14},{7,5},{8,0},{9,11},{1... | collective-permute-start | bytes 196616 | tf_op jit(solution)/shard_map/ppermute | solution.py:493
  104.9 7.3 %collective-permute-start.15 = (f32[128,128]{1,0:T(8,128)S(1)}, f32[128,128]{1,0:T(8,128)S(1)}, u32[]{:S(2)}, u32[]{:S(2)}) collective-permute-start(f32[128,128]{1,0:T(8,128)S(1)} %bitcast_add_fusion.11.token_ref), channel_id=1, source_target_pairs={{0,8},{1,3},{2,10},{3,1},{4,12},{5,7},{6,14},{7,5},{8,0},{9,11},{1... | collective-permute-start | bytes 196616 | tf_op jit(solution)/shard_map/ppermute | solution.py:493
  112.3 6.4 %collective-permute-start.18 = (f32[512,128]{1,0:T(8,128)S(1)}, f32[512,128]{1,0:T(8,128)S(1)}, u32[]{:S(2)}, u32[]{:S(2)}) collective-permute-start(f32[512,128]{1,0:T(8,128)S(1)} %dynamic-slice_bitcast_fusion), channel_id=1, source_target_pairs={{0,2},{1,5},{2,0},{3,7},{4,6},{5,1},{6,4},{7,3},{8,10},{9,13},{10,... | collective-permute-start | bytes 786440 | tf_op jit(solution)/shard_map/ppermute | solution.py:493
  113.3 6.5 %collective-permute-start.16 = (f32[256,128]{1,0:T(8,128)S(1)}, f32[256,128]{1,0:T(8,128)S(1)}, u32[]{:S(2)}, u32[]{:S(2)}) collective-permute-start(f32[256,128]{1,0:T(8,128)S(1)} %maximum_select_fusion.14), channel_id=1, source_target_pairs={{0,4},{1,9},{2,6},{3,11},{4,0},{5,13},{6,2},{7,15},{8,12},{9,1},{1... | collective-permute-start | bytes 393224 | tf_op jit(solution)/shard_map/ppermute | solution.py:493
  119.8 6.4 %collective-permute-start.17 = (f32[512,128]{1,0:T(8,128)S(1)}, f32[512,128]{1,0:T(8,128)S(1)}, u32[]{:S(2)}, u32[]{:S(2)}) collective-permute-start(f32[512,128]{1,0:T(8,128)S(1)} %maximum_select_fusion.9), channel_id=1, source_target_pairs={{0,2},{1,5},{2,0},{3,7},{4,6},{5,1},{6,4},{7,3},{8,10},{9,13},{10,... | collective-permute-start | bytes 786440 | tf_op jit(solution)/shard_map/ppermute | solution.py:493
  123.9 5.4 %collective-permute-start.20 = (f32[128,128]{1,0:T(8,128)S(1)}, f32[128,128]{1,0:T(8,128)S(1)}, u32[]{:S(2)}, u32[]{:S(2)}) collective-permute-start(f32[128,128]{1,0:T(8,128)S(1)} %dynamic-slice_bitcast_fusion.10), channel_id=1, source_target_pairs={{0,8},{1,3},{2,10},{3,1},{4,12},{5,7},{6,14},{7,5},{8,0},{9,11},{1... | collective-permute-start | bytes 196616 | tf_op jit(solution)/shard_map/ppermute | solution.py:493
  129.3 5.8 %collective-permute-start.21 = (f32[128,128]{1,0:T(8,128)S(1)}, f32[128,128]{1,0:T(8,128)S(1)}, u32[]{:S(2)}, u32[]{:S(2)}) collective-permute-start(f32[128,128]{1,0:T(8,128)S(1)} %bitcast_add_fusion.10.token_ref), channel_id=1, source_target_pairs={{0,8},{1,3},{2,10},{3,1},{4,12},{5,7},{6,14},{7,5},{8,0},{9,11},{1... | collective-permute-start | bytes 196616 | tf_op jit(solution)/shard_map/ppermute | solution.py:493
  135.2 15.6 %collective-permute-start.22 = (f32[256,128]{1,0:T(8,128)S(1)}, f32[256,128]{1,0:T(8,128)S(1)}, u32[]{:S(2)}, u32[]{:S(2)}) collective-permute-start(f32[256,128]{1,0:T(8,128)S(1)} %maximum_select_fusion.15.refs_5_), channel_id=1, source_target_pairs={{0,4},{1,9},{2,6},{3,11},{4,0},{5,13},{6,2},{7,15},{8,12},{9,1},{1... | collective-permute-start | bytes 393224 | tf_op jit(solution)/shard_map/ppermute | solution.py:493
  150.7 6.4 %collective-permute-start.23 = (f32[512,128]{1,0:T(8,128)S(1)}, f32[512,128]{1,0:T(8,128)S(1)}, u32[]{:S(2)}, u32[]{:S(2)}) collective-permute-start(f32[512,128]{1,0:T(8,128)S(1)} %maximum_select_fusion.10), channel_id=1, source_target_pairs={{0,2},{1,5},{2,0},{3,7},{4,6},{5,1},{6,4},{7,3},{8,10},{9,13},{10,... | collective-permute-start | bytes 786440 | tf_op jit(solution)/shard_map/ppermute | solution.py:493
  150.8 30.6 %collective-permute-start.24 = (f32[4096,128]{1,0:T(8,128)}, f32[4096,128]{1,0:T(8,128)S(1)}, u32[]{:S(2)}, u32[]{:S(2)}) collective-permute-start(f32[4096,128]{1,0:T(8,128)} %shard_map.54.token_ref.own0), channel_id=1, source_target_pairs={{0,1},{1,0},{2,3},{3,2},{4,5},{5,4},{6,7},{7,6},{8,9},{9,8},{10,11... | collective-permute-start | bytes 6291464 | tf_op jit(solution)/shard_map/ppermute | solution.py:518
  213.4 5.8 %collective-permute-start.29 = (f32[80,128]{1,0:T(8,128)S(1)}, f32[80,128]{1,0:T(8,128)S(1)}, u32[]{:S(2)}, u32[]{:S(2)}) collective-permute-start(f32[80,128]{1,0:T(8,128)S(1)} %bitcast_add_fusion.14), channel_id=1, source_target_pairs={{0,8},{1,3},{2,10},{3,1},{4,12},{5,7},{6,14},{7,5},{8,0},{9,11},{1... | collective-permute-start | bytes 122888 | tf_op jit(solution)/shard_map/ppermute | solution.py:493
  (13 other events, 50.8 us)
where the time goes:
time: 281 us; the launch traced here: 276 us
  Pallas kernels  165 us (59%)
  waiting for transfers between devices  71.4 us (25%)
  starting transfers between devices  31 us (11%)
  local copies, waits for them, and re-layouts  4.56 us (2%)
    ppermute x30, waiting for transfers between devices, start(): self.arriving = lax.ppermute(self.sent, ('asset', 'sample'), pairs)  69.9 us
    pallas_call x6, Pallas kernels, project(): call(project_kernel, (steps,), [pl.BlockSpec((1, length, width), lambda i...  36 us
    pallas_call x1, Pallas kernels, final_iterations(): pl.pallas_call(functools.partial(final_kernel, width_all), out_shape=(out...  35.8 us
    pallas_call x6, Pallas kernels, apply(): call(apply_kernel, (rows // width,), [block, block, pl.BlockSpec((size, l...  32.1 us
    ppermute x30, starting transfers between devices, start(): self.arriving = lax.ppermute(self.sent, ('asset', 'sample'), pairs)  30.7 us
    pallas_call x2, Pallas kernels, expand(): call(expand_kernel, (steps * slices,), [*blocks, pl.BlockSpec((size, leng...  24.4 us
    pallas_call x2, Pallas kernels, partial_grams(): call(body, (rows // height,), [pl.BlockSpec((height, size), lambda i: (i,...  18 us
    pallas_call x2, Pallas kernels, normalise(): pl.pallas_call(functools.partial(normal_kernel, width_all), in_specs=[who...  10.9 us
  transfers between devices with their start and end apart: 34, of which 20 were waited for; matrix products, arithmetic and copies ran while one was open for 1% of the time, Pallas kernels for 33%

commit v1 on v0

--- a/solution.py
+++ b/solution.py
@@ -15,6 +15,7 @@
 TILE = 8
 PANEL = 4
 WIDTH = 512
+PART = 256
 ROWS = 1024
 MEGA = 1024 * 1024
 
@@ -102,7 +103,7 @@
     return lax.dot_general(left, right, (dims, ((), ())), preferred_element_type=jnp.float32)
 
 
-def call(body, grid, in_specs, out_specs, out_shape, scratch, flops, read):
+def call(body, grid, in_specs, out_specs, out_shape, scratch, flops, read, aliases={}):
     return pl.pallas_call(
         body,
         grid=grid,
@@ -110,6 +111,7 @@
         out_specs=out_specs,
         out_shape=out_shape,
         scratch_shapes=scratch,
+        input_output_aliases=aliases,
         compiler_params=pltpu.CompilerParams(vmem_limit_bytes=52 * MEGA),
         cost_estimate=pl.CostEstimate(flops=flops, bytes_accessed=read, transcendentals=0),
     )
@@ -118,7 +120,7 @@
 TOKEN = pl.BlockSpec(memory_space=pl.ANY)
 
 
-def project_kernel(x_ref, panel_ref, token_ref, out_ref, high_ref, low_ref, total):
+def project_kernel(x_ref, panel_ref, token_ref, out_ref, total):
     step = pl.program_id(0)
     size = panel_ref.shape[1]
 
@@ -127,8 +129,6 @@
         total[...] = jnp.zeros_like(total)
 
     high, low = split(x_ref[0])
-    high_ref[...] = high
-    low_ref[...] = low
     panel_high, panel_low = split(panel_ref[...])
     sides = jnp.concatenate(
         [
@@ -150,7 +150,6 @@
     width = min(WIDTH, rows)
     steps = rows // width // slices
     first = steps * index
-    halves = jax.ShapeDtypeStruct((length, steps * width), jnp.bfloat16)
     return call(
         project_kernel,
         (steps,),
@@ -159,15 +158,11 @@
             pl.BlockSpec((width, size), lambda i: (first + i, 0)),
             TOKEN,
         ],
-        (
-            pl.BlockSpec((size, length), lambda i: (0, 0)),
-            pl.BlockSpec((length, width), lambda i: (0, i)),
-            pl.BlockSpec((length, width), lambda i: (0, i)),
-        ),
-        (jax.ShapeDtypeStruct((size, length), jnp.float32), halves, halves),
+        pl.BlockSpec((size, length), lambda i: (0, 0)),
+        jax.ShapeDtypeStruct((size, length), jnp.float32),
         [pltpu.VMEM((length, 2 * size), jnp.float32)],
         8 * length * steps * width * size,
-        8 * length * steps * width,
+        4 * length * steps * width,
     )(samples, panel, token)
 
 
@@ -177,7 +172,7 @@
     return (both[:size] + both[size:]) + dot_short(pair[:size], low)
 
 
-def apply_kernel(high_ref, low_ref, scores_ref, token_ref, out_ref, pair, total):
+def apply_kernel(x_ref, scores_ref, token_ref, out_ref, pair, total):
     step = pl.program_id(0)
     size = scores_ref.shape[0]
 
@@ -186,83 +181,89 @@
         pair[...] = jnp.concatenate(split(scores_ref[...]), axis=0)
         total[...] = jnp.zeros_like(total)
 
-    high, low = high_ref[...], low_ref[...]
-    top, rest = split(expand_part(pair[...], high, low))
+    width = x_ref.shape[2]
+    part = min(PART, width)
+    halves = [split(x_ref[0, :, at : at + part]) for at in range(0, width, part)]
+    expanded = [split(expand_part(pair[...], high, low)) for high, low in halves]
+    tops = [top for top, _ in expanded]
+    rests = [rest for _, rest in expanded]
     sides = jnp.concatenate(
         [
-            jnp.concatenate([top, rest], axis=0),
-            jnp.concatenate([top, jnp.zeros_like(rest)], axis=0),
+            jnp.concatenate(tops + tops, axis=1),
+            jnp.concatenate(rests + [jnp.zeros_like(rest) for rest in rests], axis=1),
         ],
-        axis=1,
-    )
-    total[...] += dot_short(jnp.concatenate([high, low], axis=1), sides, ((1,), (1,)))
+        axis=0,
+    )
+    left = jnp.concatenate([high for high, _ in halves] + [low for _, low in halves], axis=1)
+    total[...] += dot_short(left, sides, ((1,), (1,)))
 
     @pl.when(step == pl.num_programs(0) - 1)
     def _():
         out_ref[...] = total[:, :size] + total[:, size:]
 
 
-def apply(halves, scores, token):
-    length, rows = halves[0].shape
+def apply(samples, group, scores, slices, index, token):
+    _, length, rows = samples.shape
     size = scores.shape[0]
     width = min(WIDTH, rows)
-    block = pl.BlockSpec((length, width), lambda i: (0, i))
+    steps = rows // width // slices
+    first = steps * index
     return call(
         apply_kernel,
-        (rows // width,),
-        [block, block, pl.BlockSpec((size, length), lambda i: (0, 0)), TOKEN],
+        (steps,),
+        [
+            pl.BlockSpec((1, length, width), lambda i: (group, 0, first + i)),
+            pl.BlockSpec((size, length), lambda i: (0, 0)),
+            TOKEN,
+        ],
         pl.BlockSpec((length, size), lambda i: (0, 0)),
         jax.ShapeDtypeStruct((length, size), jnp.float32),
         [
             pltpu.VMEM((2 * size, length), jnp.bfloat16),
             pltpu.VMEM((length, 2 * size), jnp.float32),
         ],
-        16 * length * rows * size,
-        4 * length * rows,
-    )(*halves, scores, token)
-
-
-def expand_kernel(*refs):
-    *halves, scores_ref, token_ref, out_ref, pair = refs
-    step = pl.program_id(0)
-
-    @pl.when(step == 0)
+        16 * length * steps * width * size,
+        4 * length * steps * width,
+    )(samples, scores, token)
+
+
+def expand_kernel(x_ref, scores_ref, token_ref, *rest):
+    out_ref, pair = rest[-2:]
+
+    @pl.when(pl.program_id(0) == 0)
     def _():
         pair[...] = jnp.concatenate(split(scores_ref[...]), axis=0)
 
-    slices = len(halves) // 2
-    for index in range(slices):
-
-        @pl.when(step // (pl.num_programs(0) // slices) == index)
-        def _():
-            high, low = halves[2 * index][...], halves[2 * index + 1][...]
-            out_ref[...] = expand_part(pair[...], high, low).T
-
-
-def expand(halves, scores, token):
-    slices = len(halves)
-    length, held = halves[0][0].shape
+    width = x_ref.shape[2]
+    part = min(PART, width)
+    for at in range(0, width, part):
+        high, low = split(x_ref[0, :, at : at + part])
+        out_ref[at : at + part] = expand_part(pair[...], high, low).T
+
+
+def expand(samples, group, scores, slices, index, token, before=None):
+    _, length, rows = samples.shape
     size = scores.shape[0]
-    width = min(WIDTH, held)
-    steps = held // width
-    blocks = [
-        pl.BlockSpec(
-            (length, width),
-            lambda i, index=index: (0, jnp.clip(i - index * steps, 0, steps - 1)),
-        )
-        for index in range(slices)
-        for _ in range(2)
-    ]
+    width = min(WIDTH, rows)
+    steps = rows // width // slices
+    first = steps * index
+    earlier = [] if before is None else [before]
     return call(
         expand_kernel,
-        (steps * slices,),
-        [*blocks, pl.BlockSpec((size, length), lambda i: (0, 0)), TOKEN],
-        pl.BlockSpec((width, size), lambda i: (i, 0)),
-        jax.ShapeDtypeStruct((held * slices, size), jnp.float32),
+        (steps,),
+        [
+            pl.BlockSpec((1, length, width), lambda i: (group, 0, first + i)),
+            pl.BlockSpec((size, length), lambda i: (0, 0)),
+            TOKEN,
+            *[TOKEN for _ in earlier],
+        ],
+        pl.BlockSpec((width, size), lambda i: (first + i, 0)),
+        jax.ShapeDtypeStruct((rows, size), jnp.float32),
         [pltpu.VMEM((2 * size, length), jnp.bfloat16)],
-        8 * length * held * slices * size,
-        4 * length * held * slices,
-    )(*[half for pair in halves for half in pair], scores, token)
+        8 * length * steps * width * size,
+        4 * length * steps * width,
+        {3: 0} if earlier else {},
+    )(samples, scores, token, *earlier)
 
 
 def normal_kernel(width_all, first_ref, second_ref, token_ref, out_ref):
@@ -302,27 +303,30 @@
     out_ref[2] += gram[size:, size:]
 
 
-def cross_gram_kernel(own0, own1, other0, other1, out_ref):
-    @pl.when(pl.program_id(0) == 0)
-    def _():
-        out_ref[...] = jnp.zeros_like(out_ref)
+def cross_gram_kernel(own0, own1, other0, other1, out_ref, total):
+    step = pl.program_id(0)
+
+    @pl.when(step == 0)
+    def _():
+        total[...] = jnp.zeros_like(total)
 
     size = own0.shape[1]
-    swapped = lax.rem(lax.axis_index("sample"), 2) == 1
-    c, d = other0[...], other1[...]
-    pairs = ((own0[...], jnp.where(swapped, d, c)), (own1[...], jnp.where(swapped, c, d)))
-    for k, (left, right) in enumerate(pairs):
-        both = dot_short(
-            jnp.concatenate(split(left), axis=1),
-            jnp.concatenate(split(right), axis=1),
-            ((0,), (0,)),
-        )
-        out_ref[k] += (both[:size, :size] + both[size:, size:]) + (
-            both[:size, size:] + both[size:, :size]
-        )
-
-
-def partial_grams(body, count, panels):
+    first = ((0,), (0,))
+    high, low = split(jnp.concatenate([own0[...], own1[...]], axis=1))
+    right, rest = split(jnp.concatenate([other0[...], other1[...]], axis=1))
+    both = dot_short(high, jnp.concatenate([right, rest], axis=1), first)
+    total[...] += both[:, : 2 * size] + (both[:, 2 * size :] + dot_short(low, right, first))
+
+    @pl.when(step == pl.num_programs(0) - 1)
+    def _():
+        swapped = lax.rem(lax.axis_index("sample"), 2) == 1
+        pick = lambda rows, a, b: jnp.where(swapped, total[rows, b], total[rows, a])
+        front, back = slice(0, size), slice(size, 2 * size)
+        out_ref[0] = pick(front, front, back)
+        out_ref[1] = pick(back, back, front)
+
+
+def partial_grams(body, count, panels, scratch):
     rows, size = panels[0].shape
     height = min(ROWS, rows)
     return call(
@@ -331,7 +335,7 @@
         [pl.BlockSpec((height, size), lambda i: (i, 0))] * len(panels),
         pl.BlockSpec((count, size, size), lambda i: (0, 0, 0)),
         jax.ShapeDtypeStruct((count, size, size), jnp.float32),
-        [],
+        scratch,
         2 * 30 * rows * size * size,
         4 * len(panels) * rows * size,
     )(*panels)
@@ -511,6 +515,20 @@
         return self.held.reshape(self.shape)
 
 
+def total_small(value):
+    count, cores = lax.axis_size("asset"), lax.axis_size("sample")
+    bits = count.bit_length() - 1
+    orders = [list(range(bits)), list(range(1, bits)) + [0]]
+    for stage in range(bits):
+        pairs = [
+            (a * cores + c, (a ^ (1 << orders[c % 2][stage])) * cores + c)
+            for a in range(count)
+            for c in range(cores)
+        ]
+        value = value + lax.ppermute(value, ("asset", "sample"), pairs)
+    return value
+
+
 def shards(samples, start_panel):
     rows, size = start_panel.shape
     width_all = rows * lax.axis_size("asset")
@@ -518,54 +536,53 @@
     swap = lambda held: lax.ppermute(held, "sample", [(0, 1), (1, 0)])
     steps = rows // min(WIDTH, rows)
     slices = next(n for n in (4, 2, 1) if steps % n == 0)
-
-    def beside(result, total):
+    few = min(2, slices)
+    none = jnp.zeros((8, 128), jnp.float32)
+    added = lambda values: functools.reduce(jnp.add, values)
+
+    def beside(run, total):
+        result = run(total.sent)
         if total.round < total.rounds:
             result, total.arriving = lax.optimization_barrier((result, total.arriving))
+            total.step()
         return result
 
-    def in_slices(run, total):
-        done = []
-        for index in range(slices):
-            if index and total.round < total.rounds:
-                total.step()
-            done.append(beside(run(index, total.sent), total))
-        return done
-
-    none = jnp.zeros((8, 128), jnp.float32)
-    added = lambda values: functools.reduce(jnp.add, values)
-    parts0 = [project(samples, 0, start_panel, 2, k, none) for k in range(2)]
-    first0 = Total(added([part[0] for part in parts0]))
-    parts1 = in_slices(
-        lambda k, token: project(samples, 1, start_panel, slices, k, token), first0
-    )
-    first1 = Total(added([part[0] for part in parts1]))
-    while first0.round < first0.rounds:
-        first0.step()
-        if first1.round < first1.rounds:
-            first1.step()
-    halves0 = [part[1:] for part in parts0]
-    halves1 = [part[1:] for part in parts1]
+    def step_both(leading, trailing, rounds):
+        while leading.round < leading.rounds:
+            leading.step()
+            if trailing.round < rounds:
+                trailing.step()
+
+    first0 = Total(project(samples, 0, start_panel, 1, 0, none))
+    parts = [
+        beside(lambda token: project(samples, 1, start_panel, few, k, token), first0)
+        for k in range(few)
+    ]
+    first1 = Total(added(parts))
+    step_both(first0, first1, first1.rounds - slices)
     scores0 = first0.finish()
-    pieces = []
-    for k, half in enumerate(halves0):
-        pieces.append(beside(apply(half, scores0, first1.sent), first1))
-        first1.step() if first1.round < first1.rounds else None
+    parts = [
+        beside(lambda token: apply(samples, 0, scores0, slices, k, token), first1)
+        for k in range(slices)
+    ]
+    second0 = Total(added(parts))
     scores1 = first1.finish()
-    second0 = Total(added(pieces))
-    second1 = Total(
-        added(in_slices(lambda k, token: apply(halves1[k], scores1, token), second0))
-    )
-    while second0.round < second0.rounds:
-        second0.step()
-        if second1.round < second1.rounds - 2:
-            second1.step()
-    normal0 = beside(normalise(scores0, second0.finish(), width_all, second1.sent), second1)
-    second1.step()
-    own0 = beside(expand(halves0, normal0, second1.sent), second1)
+    parts = [
+        beside(lambda token: apply(samples, 1, scores1, slices, k, token), second0)
+        for k in range(slices)
+    ]
+    second1 = Total(added(parts))
+    step_both(second0, second1, 2)
+    following0 = second0.finish()
+    normal0 = beside(lambda token: normalise(scores0, following0, width_all, token), second1)
+    own0 = None
+    for k in range(few):
+        own0 = beside(
+            lambda token: expand(samples, 0, normal0, few, k, token, own0), second1
+        )
     other0 = swap(own0)
-    normal1 = normalise(scores1, second1.finish(), width_all, own0)
-    own1 = expand(halves1, normal1, none)
+    normal1 = normalise(scores1, second1.finish(), width_all, none)
+    own1 = expand(samples, 1, normal1, 1, 0, none)
     other1 = swap(own1)
     starts = jnp.einsum(
         "gks,gls->gkl",
@@ -574,13 +591,10 @@
         precision=HIGH,
     )
     other_starts = swap(starts)
-    grams = jnp.concatenate(
-        [
-            partial_grams(own_gram_kernel, 3, (own0, own1)),
-            partial_grams(cross_gram_kernel, 2, (own0, own1, other0, other1)),
-        ]
-    )
-    grams = Total(grams).finish()
+    own_grams = partial_grams(own_gram_kernel, 3, (own0, own1), [])
+    wide = pltpu.VMEM((2 * size, 2 * size), jnp.float32)
+    cross_grams = partial_grams(cross_gram_kernel, 2, (own0, own1, other0, other1), [wide])
+    grams = total_small(jnp.concatenate([own_grams, cross_grams]))
     other_grams = swap(grams)
     ordered = lambda a, b: (jnp.where(core == 0, a, b), jnp.where(core == 0, b, a))
     inverses, weights = final_iterations(

time: 281 us -> 265 us (0.943)
  Pallas kernels: 165 us -> 156 us
  waiting for transfers between devices: 71.4 us -> 67.9 us
    ppermute x30 -> x24, waiting for transfers between devices: 69.9 us -> 43.1 us  [start(): self.arriving = lax.ppermute(self.sent, ('asset', 'sample'), pairs)]
    ppermute x0 -> x3, waiting for transfers between devices: none -> 23.2 us  [total_small(): value = value + lax.ppermute(value, ('asset', 'sample'), pairs)]
    pallas_call x6 -> x3, Pallas kernels: 36 us -> 22.5 us  [project(): call(project_kernel, (steps,), [pl.BlockSpec((1, length, width), lambda i...]
    pallas_call x8 -> x11, Pallas kernels: 56.5 us -> 69.3 us  [the longest x8 35.4 us: apply(): call(apply_kernel, (steps,), [pl.BlockSpec((1, length, width), lambda i:...]
    pallas_call x2, Pallas kernels: 18 us -> 9.52 us  [partial_grams(): call(body, (rows // height,), [pl.BlockSpec((height, size), lambda i: (i,...]
    ppermute x30 -> x24, starting transfers between devices: 30.7 us -> 26.2 us  [start(): self.arriving = lax.ppermute(self.sent, ('asset', 'sample'), pairs)]
    ppermute x0 -> x3, starting transfers between devices: none -> 4.07 us  [total_small(): value = value + lax.ppermute(value, ('asset', 'sample'), pairs)]
  transfers between devices with their start and end apart: 34 -> 31, of which waited for: 20 -> 19; matrix products, arithmetic and copies ran while one was open for 1% -> 1% of each run, Pallas kernels for 33% -> 37%
where the time goes in v1:
time: 265 us; the launch traced here: 261 us
  Pallas kernels  156 us (59%)
  waiting for transfers between devices  67.9 us (26%)
  starting transfers between devices  30.4 us (11%)
  local copies, waits for them, and re-layouts  2.92 us (1%)
    ppermute x24, waiting for transfers between devices, start(): self.arriving = lax.ppermute(self.sent, ('asset', 'sample'), pairs)  43.1 us
    pallas_call x1, Pallas kernels, final_iterations(): pl.pallas_call(functools.partial(final_kernel, width_all), out_shape=(out...  35.8 us
    pallas_call x8, Pallas kernels, apply(): call(apply_kernel, (steps,), [pl.BlockSpec((1, length, width), lambda i:...  35.4 us
    pallas_call x3, Pallas kernels, expand(): call(expand_kernel, (steps,), [pl.BlockSpec((1, length, width), lambda i:...  34 us
    ppermute x24, starting transfers between devices, start(): self.arriving = lax.ppermute(self.sent, ('asset', 'sample'), pairs)  26.2 us
    ppermute x3, waiting for transfers between devices, total_small(): value = value + lax.ppermute(value, ('asset', 'sample'), pairs)  23.2 us
    pallas_call x3, Pallas kernels, project(): call(project_kernel, (steps,), [pl.BlockSpec((1, length, width), lambda i...  22.5 us
    pallas_call x2, Pallas kernels, normalise(): pl.pallas_call(functools.partial(normal_kernel, width_all), in_specs=[who...  10.9 us
  transfers between devices with their start and end apart: 31, of which 19 were waited for; matrix products, arithmetic and copies ran while one was open for 1% of the time, Pallas kernels for 37%

profile of v1, /device:TPU:0, one launch (start us, length us, event | category | flops | bytes accessed | tf_op | source)
XLA Modules:
  0.0 261.3 jit_solution(1780166973188208247)
XLA Ops:
  0.7 10.8 %shard_map.41 = f32[128,1024]{1,0:T(8,128)S(1)} custom-call(f32[2,1024,4096]{2,1,0:T(8,128)} %x_ref.27, f32[4096,128]{1,0:T(8,128)} %panel_ref.5, f32[8,128]{1,0:T(8,128)S(1)} %broadcast_in_dim.3.token_ref), custom_call_target="tpu_custom_call" | custom-call | flops 4294967296 | bytes 16777216 | tf_op jit(solution)/shard_map/pallas_call | solution.py:153
  14.6 5.8 %shard_map.42 = f32[128,1024]{1,0:T(8,128)S(1)} custom-call(f32[2,1024,4096]{2,1,0:T(8,128)} %x_ref.27, f32[4096,128]{1,0:T(8,128)} %panel_ref.5, f32[64,1024]{1,0:T(8,128)S(1)} %dynamic-slice_bitcast_fusion.3.token_ref), custom_call_target="tpu_custom_call" | custom-call | flops 2147483648 | bytes 8388608 | tf_op jit(solution)/shard_map/pallas_call | solution.py:153
  22.1 5.8 %shard_map.43 = f32[128,1024]{1,0:T(8,128)S(1)} custom-call(f32[2,1024,4096]{2,1,0:T(8,128)} %x_ref.27, f32[4096,128]{1,0:T(8,128)} %panel_ref.5, f32[32,1024]{1,0:T(8,128)S(1)} %dynamic-slice_bitcast_fusion.7.token_ref), custom_call_target="tpu_custom_call" | custom-call | flops 2147483648 | bytes 8388608 | tf_op jit(solution)/shard_map/pallas_call | solution.py:153
  36.7 6.5 %collective-permute-done.3 = f32[16,1024]{1,0:T(8,128)S(1)} collective-permute-done((f32[16,1024]{1,0:T(8,128)S(1)}, f32[16,1024]{1,0:T(8,128)S(1)}, u32[]{:S(2)}, u32[]{:S(2)}) %collective-permute-start.3) | collective-permute-done | bytes 65568 | tf_op jit(solution)/shard_map/ppermute | solution.py:497
  56.2 4.4 %shard_map.44 = f32[1024,128]{1,0:T(8,128)S(1)} custom-call(f32[2,1024,4096]{2,1,0:T(8,128)} %x_ref.27, f32[128,1024]{1,0:T(8,128)S(1)} %maximum_select_fusion.scores_ref.first_ref, f32[16,1024]{1,0:T(8,128)S(1)} %dynamic-slice_bitcast_fusion.10.token_ref), custom_call_target="tpu_custom_call" | custom-call | flops 2147483648 | bytes 4194304 | tf_op jit(solution)/shard_map/pallas_call | solution.py:211
  61.3 4.4 %shard_map.45 = f32[1024,128]{1,0:T(8,128)S(1)} custom-call(f32[2,1024,4096]{2,1,0:T(8,128)} %x_ref.27, f32[128,1024]{1,0:T(8,128)S(1)} %maximum_select_fusion.scores_ref.first_ref, f32[16,1024]{1,0:T(8,128)S(1)} %bitcast_add_fusion.10.token_ref), custom_call_target="tpu_custom_call" | custom-call | flops 2147483648 | bytes 4194304 | tf_op jit(solution)/shard_map/pallas_call | solution.py:211
  68.2 4.4 %shard_map.46 = f32[1024,128]{1,0:T(8,128)S(1)} custom-call(f32[2,1024,4096]{2,1,0:T(8,128)} %x_ref.27, f32[128,1024]{1,0:T(8,128)S(1)} %maximum_select_fusion.scores_ref.first_ref, f32[32,1024]{1,0:T(8,128)S(1)} %maximum_select_fusion.11.token_ref), custom_call_target="tpu_custom_call" | custom-call | flops 2147483648 | bytes 4194304 | tf_op jit(solution)/shard_map/pallas_call | solution.py:211
  74.6 4.4 %shard_map.47 = f32[1024,128]{1,0:T(8,128)S(1)} custom-call(f32[2,1024,4096]{2,1,0:T(8,128)} %x_ref.27, f32[128,1024]{1,0:T(8,128)S(1)} %maximum_select_fusion.scores_ref.first_ref, f32[64,1024]{1,0:T(8,128)S(1)} %maximum_select_fusion.7.token_ref), custom_call_target="tpu_custom_call" | custom-call | flops 2147483648 | bytes 4194304 | tf_op jit(solution)/shard_map/pallas_call | solution.py:211
  81.2 4.4 %shard_map.48 = f32[1024,128]{1,0:T(8,128)S(1)} custom-call(f32[2,1024,4096]{2,1,0:T(8,128)} %x_ref.27, f32[128,1024]{1,0:T(8,128)S(1)} %maximum_select_fusion.1.scores_ref.first_ref, f32[512,128]{1,0:T(8,128)S(1)} %dynamic-slice_bitcast_fusion.1.token_ref), custom_call_target="tpu_custom_call" | custom-call | flops 2147483648 | bytes 4194304 | tf_op jit(solution)/shard_map/pallas_call | solution.py:211
  87.8 4.4 %shard_map.49 = f32[1024,128]{1,0:T(8,128)S(1)} custom-call(f32[2,1024,4096]{2,1,0:T(8,128)} %x_ref.27, f32[128,1024]{1,0:T(8,128)S(1)} %maximum_select_fusion.1.scores_ref.first_ref, f32[256,128]{1,0:T(8,128)S(1)} %dynamic-slice_bitcast_fusion.5.token_ref), custom_call_target="tpu_custom_call" | custom-call | flops 2147483648 | bytes 4194304 | tf_op jit(solution)/shard_map/pallas_call | solution.py:211
  94.0 4.6 %shard_map.50 = f32[1024,128]{1,0:T(8,128)S(1)} custom-call(f32[2,1024,4096]{2,1,0:T(8,128)} %x_ref.27, f32[128,1024]{1,0:T(8,128)S(1)} %maximum_select_fusion.1.scores_ref.first_ref, f32[128,128]{1,0:T(8,128)S(1)} %dynamic-slice_bitcast_fusion.9.token_ref), custom_call_target="tpu_custom_call" | custom-call | flops 2147483648 | bytes 4194304 | tf_op jit(solution)/shard_map/pallas_call | solution.py:211
  100.4 4.4 %shard_map.51 = f32[1024,128]{1,0:T(8,128)S(1)} custom-call(f32[2,1024,4096]{2,1,0:T(8,128)} %x_ref.27, f32[128,1024]{1,0:T(8,128)S(1)} %maximum_select_fusion.1.scores_ref.first_ref, f32[128,128]{1,0:T(8,128)S(1)} %bitcast_add_fusion.9.token_ref), custom_call_target="tpu_custom_call" | custom-call | flops 2147483648 | bytes 4194304 | tf_op jit(solution)/shard_map/pallas_call | solution.py:211
  120.4 5.4 %shard_map.52.scores_ref = f32[128,1024]{1,0:T(8,128)S(1)} custom-call(f32[128,1024]{1,0:T(8,128)S(1)} %maximum_select_fusion.scores_ref.first_ref, f32[1024,128]{1,0:T(8,128)S(1)} %maximum_select_fusion.2.second_ref, f32[128,128]{1,0:T(8,128)S(1)} %dynamic-slice_bitcast_fusion.8.token_ref), custom_call_target="tpu_custom_call" | custom-call | flops 6000000000 | bytes 1572864 | tf_op jit(solution)/shard_map/pallas_call | solution.py:278
  127.7 6.4 %shard_map.53.rest_0_ = f32[4096,128]{1,0:T(8,128)} custom-call(f32[2,1024,4096]{2,1,0:T(8,128)} %x_ref.27, f32[128,1024]{1,0:T(8,128)S(1)} %shard_map.52.scores_ref, f32[128,128]{1,0:T(8,128)S(1)} %bitcast_add_fusion.8.token_ref), custom_call_target="tpu_custom_call" | custom-call | flops 2147483648 | bytes 8388608 | tf_op jit(solution)/shard_map/pallas_call | solution.py:251
  134.6 6.4 %shard_map.54.own0 = f32[4096,128]{1,0:T(8,128)} custom-call(f32[2,1024,4096]{2,1,0:T(8,128)} %x_ref.27, f32[128,1024]{1,0:T(8,128)S(1)} %shard_map.52.scores_ref, f32[256,128]{1,0:T(8,128)S(1)} %maximum_select_fusion.13.token_ref, f32[4096,128]{1,0:T(8,128)} %shard_map.53.rest_0_), custom_call_target="tpu_custom_call", output_to_operand_aliasing={{}: (3, {})} | custom-call | flops 2147483648 | bytes 8388608 | tf_op jit(solution)/shard_map/pallas_call | solution.py:251
  141.9 5.5 %collective-permute-done.23 = f32[512,128]{1,0:T(8,128)S(1)} collective-permute-done((f32[512,128]{1,0:T(8,128)S(1)}, f32[512,128]{1,0:T(8,128)S(1)}, u32[]{:S(2)}, u32[]{:S(2)}) %collective-permute-start.23) | collective-permute-done | bytes 262176 | tf_op jit(solution)/shard_map/ppermute | solution.py:497
  147.5 5.4 %shard_map.55.scores_ref = f32[128,1024]{1,0:T(8,128)S(1)} custom-call(f32[128,1024]{1,0:T(8,128)S(1)} %maximum_select_fusion.1.scores_ref.first_ref, f32[1024,128]{1,0:T(8,128)S(1)} %maximum_select_fusion.3.second_ref, f32[8,128]{1,0:T(8,128)S(1)} %broadcast_in_dim.3.token_ref), custom_call_target="tpu_custom_call" | custom-call | flops 6000000000 | bytes 1572864 | tf_op jit(solution)/shard_map/pallas_call | solution.py:278
  152.9 21.2 %shard_map.56.own1 = f32[4096,128]{1,0:T(8,128)} custom-call(f32[2,1024,4096]{2,1,0:T(8,128)} %x_ref.27, f32[128,1024]{1,0:T(8,128)S(1)} %shard_map.55.scores_ref, f32[8,128]{1,0:T(8,128)S(1)} %broadcast_in_dim.3.token_ref), custom_call_target="tpu_custom_call" | custom-call | flops 4294967296 | bytes 16777216 | tf_op jit(solution)/shard_map/pallas_call | solution.py:251
  181.3 5.1 %shard_map.58 = f32[2,128,128]{2,1,0:T(8,128)S(1)} custom-call(f32[4096,128]{1,0:T(8,128)} %shard_map.54.own0, f32[4096,128]{1,0:T(8,128)} %shard_map.56.own1, f32[4096,128]{1,0:T(8,128)} %copy-done, f32[4096,128]{1,0:T(8,128)} %copy-done.1), custom_call_target="tpu_custom_call" | custom-call | flops 4026531840 | bytes 8388608 | tf_op jit(solution)/shard_map/pallas_call | solution.py:332
  187.3 6.2 %collective-permute-done.26 = f32[5,128,128]{2,1,0:T(8,128)S(1)} collective-permute-done((f32[5,128,128]{2,1,0:T(8,128)S(1)}, f32[5,128,128]{2,1,0:T(8,128)S(1)}, u32[]{:S(2)}, u32[]{:S(2)}) %collective-permute-start.26) | collective-permute-done | bytes 327712 | tf_op jit(solution)/shard_map/ppermute | solution.py:528
  195.3 8.6 %collective-permute-done.27 = f32[5,128,128]{2,1,0:T(8,128)S(1)} collective-permute-done((f32[5,128,128]{2,1,0:T(8,128)S(1)}, f32[5,128,128]{2,1,0:T(8,128)S(1)}, u32[]{:S(2)}, u32[]{:S(2)}) %collective-permute-start.27) | collective-permute-done | bytes 327712 | tf_op jit(solution)/shard_map/ppermute | solution.py:528
  206.7 8.4 %collective-permute-done.28 = f32[5,128,128]{2,1,0:T(8,128)S(1)} collective-permute-done((f32[5,128,128]{2,1,0:T(8,128)S(1)}, f32[5,128,128]{2,1,0:T(8,128)S(1)}, u32[]{:S(2)}, u32[]{:S(2)}) %collective-permute-start.28) | collective-permute-done | bytes 327712 | tf_op jit(solution)/shard_map/ppermute | solution.py:528
  216.9 35.8 %shard_map.59 = (f32[4,128,128]{2,1,0:T(8,128)S(1)}, f32[4,128,128]{2,1,0:T(8,128)S(1)}) custom-call(f32[5,128,128]{2,1,0:T(8,128)S(1)} %get-tuple-element.59.first, f32[5,128,128]{2,1,0:T(8,128)S(1)} %get-tuple-element.58.second, f32[2,128,128]{2,1,0:T(8,128)S(1)} %get-tuple-element.61.start0, f32[2,128,128]{2,1,0:T(8,128)S(1)} %get-tuple-element.60.start1), custom_call_target="tpu_custom_call" | custom-call | tf_op jit(solution)/shard_map/pallas_call | solution.py:392
  252.7 8.3 %shard_map.60 = (f32[2,4096,128]{2,1,0:T(8,128)}, f32[4096,128]{1,0:T(8,128)}) custom-call(f32[4096,128]{1,0:T(8,128)} %shard_map.54.own0, f32[4096,128]{1,0:T(8,128)} %shard_map.56.own1, f32[4096,128]{1,0:T(8,128)} %copy-done, f32[4096,128]{1,0:T(8,128)} %copy-done.1, f32[4,128,128]{2,1,0:T(8,128)S(1)} %get-tuple-element.56.inverse_ref, ...), custom_call_target="tpu_custom_call" | custom-call | flops 3221225472 | bytes 14680064 | tf_op jit(solution)/shard_map/pallas_call | solution.py:443
  (111 shorter events, 72.5 us)
Async XLA Ops:
  11.5 8.9 %collective-permute-start = (f32[64,1024]{1,0:T(8,128)S(1)}, f32[64,1024]{1,0:T(8,128)S(1)}, u32[]{:S(2)}, u32[]{:S(2)}) collective-permute-start(f32[64,1024]{1,0:T(8,128)S(1)} %dynamic-slice_bitcast_fusion.3.token_ref), channel_id=1, source_target_pairs={{0,2},{1,5},{2,0},{3,7},{4,6},{5,1},{6,4},{7,3},{8,10},{9,13},{10,... | collective-permute-start | bytes 786440 | tf_op jit(solution)/shard_map/ppermute | solution.py:497
  20.5 7.5 %collective-permute-start.1 = (f32[32,1024]{1,0:T(8,128)S(1)}, f32[32,1024]{1,0:T(8,128)S(1)}, u32[]{:S(2)}, u32[]{:S(2)}) collective-permute-start(f32[32,1024]{1,0:T(8,128)S(1)} %dynamic-slice_bitcast_fusion.7.token_ref), channel_id=1, source_target_pairs={{0,4},{1,9},{2,6},{3,11},{4,0},{5,13},{6,2},{7,15},{8,12},{9,1},{1... | collective-permute-start | bytes 393224 | tf_op jit(solution)/shard_map/ppermute | solution.py:497
  30.8 12.5 %collective-permute-start.6 = (f32[64,1024]{1,0:T(8,128)S(1)}, f32[64,1024]{1,0:T(8,128)S(1)}, u32[]{:S(2)}, u32[]{:S(2)}) collective-permute-start(f32[64,1024]{1,0:T(8,128)S(1)} %dynamic-slice_bitcast_fusion.2), channel_id=1, source_target_pairs={{0,2},{1,5},{2,0},{3,7},{4,6},{5,1},{6,4},{7,3},{8,10},{9,13},{10,... | collective-permute-start | bytes 786440 | tf_op jit(solution)/shard_map/ppermute | solution.py:497
  34.0 9.2 %collective-permute-start.3 = (f32[16,1024]{1,0:T(8,128)S(1)}, f32[16,1024]{1,0:T(8,128)S(1)}, u32[]{:S(2)}, u32[]{:S(2)}) collective-permute-start(f32[16,1024]{1,0:T(8,128)S(1)} %bitcast_add_fusion.11), channel_id=1, source_target_pairs={{0,8},{1,3},{2,10},{3,1},{4,12},{5,7},{6,14},{7,5},{8,0},{9,11},{1... | collective-permute-start | bytes 196616 | tf_op jit(solution)/shard_map/ppermute | solution.py:497
  43.2 6.4 %collective-permute-start.4 = (f32[32,1024]{1,0:T(8,128)S(1)}, f32[32,1024]{1,0:T(8,128)S(1)}, u32[]{:S(2)}, u32[]{:S(2)}) collective-permute-start(f32[32,1024]{1,0:T(8,128)S(1)} %maximum_select_fusion.10), channel_id=1, source_target_pairs={{0,4},{1,9},{2,6},{3,11},{4,0},{5,13},{6,2},{7,15},{8,12},{9,1},{1... | collective-permute-start | bytes 393224 | tf_op jit(solution)/shard_map/ppermute | solution.py:497
  43.4 8.8 %collective-permute-start.7 = (f32[32,1024]{1,0:T(8,128)S(1)}, f32[32,1024]{1,0:T(8,128)S(1)}, u32[]{:S(2)}, u32[]{:S(2)}) collective-permute-start(f32[32,1024]{1,0:T(8,128)S(1)} %dynamic-slice_bitcast_fusion.6), channel_id=1, source_target_pairs={{0,4},{1,9},{2,6},{3,11},{4,0},{5,13},{6,2},{7,15},{8,12},{9,1},{1... | collective-permute-start | bytes 393224 | tf_op jit(solution)/shard_map/ppermute | solution.py:497
  49.7 6.4 %collective-permute-start.5 = (f32[64,1024]{1,0:T(8,128)S(1)}, f32[64,1024]{1,0:T(8,128)S(1)}, u32[]{:S(2)}, u32[]{:S(2)}) collective-permute-start(f32[64,1024]{1,0:T(8,128)S(1)} %maximum_select_fusion.6), channel_id=1, source_target_pairs={{0,2},{1,5},{2,0},{3,7},{4,6},{5,1},{6,4},{7,3},{8,10},{9,13},{10,... | collective-permute-start | bytes 786440 | tf_op jit(solution)/shard_map/ppermute | solution.py:497
  52.2 8.4 %collective-permute-start.8 = (f32[16,1024]{1,0:T(8,128)S(1)}, f32[16,1024]{1,0:T(8,128)S(1)}, u32[]{:S(2)}, u32[]{:S(2)}) collective-permute-start(f32[16,1024]{1,0:T(8,128)S(1)} %dynamic-slice_bitcast_fusion.10.token_ref), channel_id=1, source_target_pairs={{0,8},{1,3},{2,10},{3,1},{4,12},{5,7},{6,14},{7,5},{8,0},{9,11},{1... | collective-permute-start | bytes 196616 | tf_op jit(solution)/shard_map/ppermute | solution.py:497
  60.6 7.5 %collective-permute-start.9 = (f32[16,1024]{1,0:T(8,128)S(1)}, f32[16,1024]{1,0:T(8,128)S(1)}, u32[]{:S(2)}, u32[]{:S(2)}) collective-permute-start(f32[16,1024]{1,0:T(8,128)S(1)} %bitcast_add_fusion.10.token_ref), channel_id=1, source_target_pairs={{0,8},{1,3},{2,10},{3,1},{4,12},{5,7},{6,14},{7,5},{8,0},{9,11},{1... | collective-permute-start | bytes 196616 | tf_op jit(solution)/shard_map/ppermute | solution.py:497
  68.1 6.4 %collective-permute-start.10 = (f32[32,1024]{1,0:T(8,128)S(1)}, f32[32,1024]{1,0:T(8,128)S(1)}, u32[]{:S(2)}, u32[]{:S(2)}) collective-permute-start(f32[32,1024]{1,0:T(8,128)S(1)} %maximum_select_fusion.11.token_ref), channel_id=1, source_target_pairs={{0,4},{1,9},{2,6},{3,11},{4,0},{5,13},{6,2},{7,15},{8,12},{9,1},{1... | collective-permute-start | bytes 393224 | tf_op jit(solution)/shard_map/ppermute | solution.py:497
  74.5 6.4 %collective-permute-start.11 = (f32[64,1024]{1,0:T(8,128)S(1)}, f32[64,1024]{1,0:T(8,128)S(1)}, u32[]{:S(2)}, u32[]{:S(2)}) collective-permute-start(f32[64,1024]{1,0:T(8,128)S(1)} %maximum_select_fusion.7.token_ref), channel_id=1, source_target_pairs={{0,2},{1,5},{2,0},{3,7},{4,6},{5,1},{6,4},{7,3},{8,10},{9,13},{10,... | collective-permute-start | bytes 786440 | tf_op jit(solution)/shard_map/ppermute | solution.py:497
  81.1 6.4 %collective-permute-start.12 = (f32[512,128]{1,0:T(8,128)S(1)}, f32[512,128]{1,0:T(8,128)S(1)}, u32[]{:S(2)}, u32[]{:S(2)}) collective-permute-start(f32[512,128]{1,0:T(8,128)S(1)} %dynamic-slice_bitcast_fusion.1.token_ref), channel_id=1, source_target_pairs={{0,2},{1,5},{2,0},{3,7},{4,6},{5,1},{6,4},{7,3},{8,10},{9,13},{10,... | collective-permute-start | bytes 786440 | tf_op jit(solution)/shard_map/ppermute | solution.py:497
  104.9 6.6 %collective-permute-start.18 = (f32[512,128]{1,0:T(8,128)S(1)}, f32[512,128]{1,0:T(8,128)S(1)}, u32[]{:S(2)}, u32[]{:S(2)}) collective-permute-start(f32[512,128]{1,0:T(8,128)S(1)} %dynamic-slice_bitcast_fusion), channel_id=1, source_target_pairs={{0,2},{1,5},{2,0},{3,7},{4,6},{5,1},{6,4},{7,3},{8,10},{9,13},{10,... | collective-permute-start | bytes 786440 | tf_op jit(solution)/shard_map/ppermute | solution.py:497
  107.1 6.8 %collective-permute-start.16 = (f32[256,128]{1,0:T(8,128)S(1)}, f32[256,128]{1,0:T(8,128)S(1)}, u32[]{:S(2)}, u32[]{:S(2)}) collective-permute-start(f32[256,128]{1,0:T(8,128)S(1)} %maximum_select_fusion.12), channel_id=1, source_target_pairs={{0,4},{1,9},{2,6},{3,11},{4,0},{5,13},{6,2},{7,15},{8,12},{9,1},{1... | collective-permute-start | bytes 393224 | tf_op jit(solution)/shard_map/ppermute | solution.py:497
  113.9 6.4 %collective-permute-start.17 = (f32[512,128]{1,0:T(8,128)S(1)}, f32[512,128]{1,0:T(8,128)S(1)}, u32[]{:S(2)}, u32[]{:S(2)}) collective-permute-start(f32[512,128]{1,0:T(8,128)S(1)} %maximum_select_fusion.8), channel_id=1, source_target_pairs={{0,2},{1,5},{2,0},{3,7},{4,6},{5,1},{6,4},{7,3},{8,10},{9,13},{10,... | collective-permute-start | bytes 786440 | tf_op jit(solution)/shard_map/ppermute | solution.py:497
  116.6 9.3 %collective-permute-start.20 = (f32[128,128]{1,0:T(8,128)S(1)}, f32[128,128]{1,0:T(8,128)S(1)}, u32[]{:S(2)}, u32[]{:S(2)}) collective-permute-start(f32[128,128]{1,0:T(8,128)S(1)} %dynamic-slice_bitcast_fusion.8.token_ref), channel_id=1, source_target_pairs={{0,8},{1,3},{2,10},{3,1},{4,12},{5,7},{6,14},{7,5},{8,0},{9,11},{1... | collective-permute-start | bytes 196616 | tf_op jit(solution)/shard_map/ppermute | solution.py:497
  125.9 8.2 %collective-permute-start.21 = (f32[128,128]{1,0:T(8,128)S(1)}, f32[128,128]{1,0:T(8,128)S(1)}, u32[]{:S(2)}, u32[]{:S(2)}) collective-permute-start(f32[128,128]{1,0:T(8,128)S(1)} %bitcast_add_fusion.8.token_ref), channel_id=1, source_target_pairs={{0,8},{1,3},{2,10},{3,1},{4,12},{5,7},{6,14},{7,5},{8,0},{9,11},{1... | collective-permute-start | bytes 196616 | tf_op jit(solution)/shard_map/ppermute | solution.py:497
  134.1 6.8 %collective-permute-start.22 = (f32[256,128]{1,0:T(8,128)S(1)}, f32[256,128]{1,0:T(8,128)S(1)}, u32[]{:S(2)}, u32[]{:S(2)}) collective-permute-start(f32[256,128]{1,0:T(8,128)S(1)} %maximum_select_fusion.13.token_ref), channel_id=1, source_target_pairs={{0,4},{1,9},{2,6},{3,11},{4,0},{5,13},{6,2},{7,15},{8,12},{9,1},{1... | collective-permute-start | bytes 393224 | tf_op jit(solution)/shard_map/ppermute | solution.py:497
  141.0 6.4 %collective-permute-start.23 = (f32[512,128]{1,0:T(8,128)S(1)}, f32[512,128]{1,0:T(8,128)S(1)}, u32[]{:S(2)}, u32[]{:S(2)}) collective-permute-start(f32[512,128]{1,0:T(8,128)S(1)} %maximum_select_fusion.9), channel_id=1, source_target_pairs={{0,2},{1,5},{2,0},{3,7},{4,6},{5,1},{6,4},{7,3},{8,10},{9,13},{10,... | collective-permute-start | bytes 786440 | tf_op jit(solution)/shard_map/ppermute | solution.py:497
  141.9 36.7 %collective-permute-start.24 = (f32[4096,128]{1,0:T(8,128)}, f32[4096,128]{1,0:T(8,128)S(1)}, u32[]{:S(2)}, u32[]{:S(2)}) collective-permute-start(f32[4096,128]{1,0:T(8,128)} %shard_map.54.own0), channel_id=1, source_target_pairs={{0,1},{1,0},{2,3},{3,2},{4,5},{5,4},{6,7},{7,6},{8,9},{9,8},{10,11... | collective-permute-start | bytes 6291464 | tf_op jit(solution)/shard_map/ppermute | solution.py:536
  186.4 7.1 %collective-permute-start.26 = (f32[5,128,128]{2,1,0:T(8,128)S(1)}, f32[5,128,128]{2,1,0:T(8,128)S(1)}, u32[]{:S(2)}, u32[]{:S(2)}) collective-permute-start(f32[5,128,128]{2,1,0:T(8,128)S(1)} %pad_maximum_fusion), channel_id=1, source_target_pairs={{0,2},{1,5},{2,0},{3,7},{4,6},{5,1},{6,4},{7,3},{8,10},{9,13},{10,... | collective-permute-start | bytes 983048 | tf_op jit(solution)/shard_map/ppermute | solution.py:528
  193.6 10.2 %collective-permute-start.27 = (f32[5,128,128]{2,1,0:T(8,128)S(1)}, f32[5,128,128]{2,1,0:T(8,128)S(1)}, u32[]{:S(2)}, u32[]{:S(2)}) collective-permute-start(f32[5,128,128]{2,1,0:T(8,128)S(1)} %fusion.8), channel_id=1, source_target_pairs={{0,4},{1,9},{2,6},{3,11},{4,0},{5,13},{6,2},{7,15},{8,12},{9,1},{1... | collective-permute-start | bytes 983048 | tf_op jit(solution)/shard_map/ppermute | solution.py:528
  203.9 11.2 %collective-permute-start.28 = (f32[5,128,128]{2,1,0:T(8,128)S(1)}, f32[5,128,128]{2,1,0:T(8,128)S(1)}, u32[]{:S(2)}, u32[]{:S(2)}) collective-permute-start(f32[5,128,128]{2,1,0:T(8,128)S(1)} %add.165), channel_id=1, source_target_pairs={{0,8},{1,3},{2,10},{3,1},{4,12},{5,7},{6,14},{7,5},{8,0},{9,11},{1... | collective-permute-start | bytes 983048 | tf_op jit(solution)/shard_map/ppermute | solution.py:528
  206.6 8.6 %collective-permute-start.30 = (f32[2,128,128]{2,1,0:T(8,128)S(1)}, f32[2,128,128]{2,1,0:T(8,128)S(1)}, u32[]{:S(2)}, u32[]{:S(2)}) collective-permute-start(f32[2,128,128]{2,1,0:T(8,128)S(1)} %fusion), channel_id=1, source_target_pairs={{0,1},{1,0},{2,3},{3,2},{4,5},{5,4},{6,7},{7,6},{8,9},{9,8},{10,11... | collective-permute-start | bytes 393224 | tf_op jit(solution)/shard_map/ppermute | solution.py:536
  (9 other events, 37.0 us)

commit v2 on v1

--- a/solution.py
+++ b/solution.py
@@ -32,10 +32,23 @@
     full = (TILE, size)
     sublane = lax.broadcasted_iota(jnp.int32, full, 0)
     lane = lax.broadcasted_iota(jnp.int32, full, 1)
-    left, right = [], []
+    left, right, scales = [], [], []
     for matrix in matrices:
         symmetric = 0.5 * (matrix + matrix.T)
-        left.append([symmetric[TILE * i : TILE * (i + 1)] for i in range(blocks)])
+        rows = [symmetric[TILE * i : TILE * (i + 1)] for i in range(blocks)]
+        on_diagonal = [
+            jnp.where(lane == sublane + TILE * i, row, 0.0) for i, row in enumerate(rows)
+        ]
+        along_lanes = lax.rsqrt(jnp.sum(sum(on_diagonal), axis=0, keepdims=True))
+        scales.append(jnp.broadcast_to(along_lanes, full))
+        left.append(
+            [
+                row
+                * lax.rsqrt(jnp.broadcast_to(jnp.sum(own, axis=1, keepdims=True), full))
+                * scales[-1]
+                for row, own in zip(rows, on_diagonal)
+            ]
+        )
         right.append(
             [jnp.where(lane == sublane + TILE * i, 1.0, 0.0) for i in range(blocks)]
         )
@@ -48,13 +61,20 @@
                 columns = [across(a[j], TILE * j + k) for k in range(TILE)]
                 d = [[along(columns[k], i) for k in range(i + 1)] for i in range(TILE)]
                 scale = []
-                for k in range(TILE):
-                    scale.append(lax.rsqrt(d[k][k]))
-                    for i in range(k + 1, TILE):
+                for k in range(0, TILE, 2):
+                    corner, side, end = d[k][k], d[k + 1][k], d[k + 1][k + 1]
+                    determinant = corner * end - side * side
+                    scale.append(lax.rsqrt(corner))
+                    scale.append(lax.rsqrt(determinant) * (corner * scale[k]))
+                    d[k + 1][k] = side * scale[k]
+                    for i in range(k + 2, TILE):
                         d[i][k] = d[i][k] * scale[k]
-                    for i in range(k + 1, TILE):
-                        for m in range(k + 1, i + 1):
-                            d[i][m] = d[i][m] - d[i][k] * d[m][k]
+                        d[i][k + 1] = (d[i][k + 1] - d[i][k] * d[k + 1][k]) * scale[k + 1]
+                    for i in range(k + 2, TILE):
+                        for m in range(k + 2, i + 1):
+                            d[i][m] = d[i][m] - (
+                                d[i][k] * d[m][k] + d[i][k + 1] * d[m][k + 1]
+                            )
 
                 def substitute(parts):
                     for k in range(TILE):
@@ -91,7 +111,9 @@
                     rows = change[TILE * (i - last) : TILE * (i - last + 1)]
                     a[i] = a[i] - rows[:, :size]
                     b[i] = b[i] - rows[:, size:]
-    return [jnp.concatenate(b, axis=0) for b in right]
+    return [
+        jnp.concatenate([row * scale for row in b], axis=0) for b, scale in zip(right, scales)
+    ]
 
 
 def split(value):
@@ -103,7 +125,7 @@
     return lax.dot_general(left, right, (dims, ((), ())), preferred_element_type=jnp.float32)
 
 
-def call(body, grid, in_specs, out_specs, out_shape, scratch, flops, read, aliases={}):
+def call(body, grid, in_specs, out_specs, out_shape, scratch, flops, read, aliases={}, limit=52):
     return pl.pallas_call(
         body,
         grid=grid,
@@ -112,7 +134,7 @@
         out_shape=out_shape,
         scratch_shapes=scratch,
         input_output_aliases=aliases,
-        compiler_params=pltpu.CompilerParams(vmem_limit_bytes=52 * MEGA),
+        compiler_params=pltpu.CompilerParams(vmem_limit_bytes=limit * MEGA),
         cost_estimate=pl.CostEstimate(flops=flops, bytes_accessed=read, transcendentals=0),
     )
 
@@ -338,6 +360,7 @@
         scratch,
         2 * 30 * rows * size * size,
         4 * len(panels) * rows * size,
+        limit=60,
     )(*panels)
 
 
@@ -438,7 +461,7 @@
 
 def outputs(own, other, inverses, weights):
     rows, size = own[0].shape
-    height = min(ROWS, rows)
+    height = min(ROWS // 2, rows)
     whole = pl.BlockSpec(inverses.shape, lambda i: (0, 0, 0))
     return call(
         output_kernel,
@@ -515,18 +538,29 @@
         return self.held.reshape(self.shape)
 
 
-def total_small(value):
-    count, cores = lax.axis_size("asset"), lax.axis_size("sample")
-    bits = count.bit_length() - 1
-    orders = [list(range(bits)), list(range(1, bits)) + [0]]
-    for stage in range(bits):
+class SmallTotal:
+    def __init__(self, value):
+        self.count, self.cores = lax.axis_size("asset"), lax.axis_size("sample")
+        self.rounds = self.count.bit_length() - 1
+        bits = list(range(self.rounds))
+        self.orders = [bits, bits[1:] + bits[:1]]
+        self.held, self.round = value, 0
+        self.start()
+
+    def start(self):
         pairs = [
-            (a * cores + c, (a ^ (1 << orders[c % 2][stage])) * cores + c)
-            for a in range(count)
-            for c in range(cores)
+            (a * self.cores + c, (a ^ (1 << self.orders[c % 2][self.round])) * self.cores + c)
+            for a in range(self.count)
+            for c in range(self.cores)
         ]
-        value = value + lax.ppermute(value, ("asset", "sample"), pairs)
-    return value
+        self.sent = self.held
+        self.arriving = lax.ppermute(self.sent, ("asset", "sample"), pairs)
+
+    def step(self):
+        self.held = self.held + self.arriving
+        self.round += 1
+        if self.round < self.rounds:
+            self.start()
 
 
 def shards(samples, start_panel):
@@ -555,8 +589,8 @@
 
     first0 = Total(project(samples, 0, start_panel, 1, 0, none))
     parts = [
-        beside(lambda token: project(samples, 1, start_panel, few, k, token), first0)
-        for k in range(few)
+        beside(lambda token: project(samples, 1, start_panel, slices, k, token), first0)
+        for k in range(slices)
     ]
     first1 = Total(added(parts))
     step_both(first0, first1, first1.rounds - slices)
@@ -593,8 +627,20 @@
     other_starts = swap(starts)
     own_grams = partial_grams(own_gram_kernel, 3, (own0, own1), [])
     wide = pltpu.VMEM((2 * size, 2 * size), jnp.float32)
-    cross_grams = partial_grams(cross_gram_kernel, 2, (own0, own1, other0, other1), [wide])
-    grams = total_small(jnp.concatenate([own_grams, cross_grams]))
+    own_total = SmallTotal(own_grams)
+    cross_total = SmallTotal(
+        beside(
+            lambda token: partial_grams(
+                cross_gram_kernel, 2, (own0, own1, other0, other1), [wide]
+            ),
+            own_total,
+        )
+    )
+    while cross_total.round < cross_total.rounds:
+        if own_total.round < own_total.rounds:
+            own_total.step()
+        cross_total.step()
+    grams = jnp.concatenate([own_total.held, cross_total.held])
     other_grams = swap(grams)
     ordered = lambda a, b: (jnp.where(core == 0, a, b), jnp.where(core == 0, b, a))
     inverses, weights = final_iterations(

time: 265 us -> 255 us (0.962)
  waiting for transfers between devices: 67.9 us -> 34.6 us
  starting transfers between devices: 30.4 us -> 51 us
  Pallas kernels: 156 us -> 160 us
  local copies, waits for them, and re-layouts: 2.92 us -> 0.25 us
    ppermute x24 -> x30, starting transfers between devices: 26.2 us -> 50.8 us  [start(): self.arriving = lax.ppermute(self.sent, ('asset', 'sample'), pairs)]
    ppermute x3 -> x0, waiting for transfers between devices: 23.2 us -> none  [total_small(): value = value + lax.ppermute(value, ('asset', 'sample'), pairs)]
    ppermute x24 -> x30, waiting for transfers between devices: 43.1 us -> 33 us  [start(): self.arriving = lax.ppermute(self.sent, ('asset', 'sample'), pairs)]
    pallas_call x2, Pallas kernels: 9.52 us -> 19.3 us  [partial_grams(): call(body, (rows // height,), [pl.BlockSpec((height, size), lambda i: (i,...]
    pallas_call x3, Pallas kernels: 34 us -> 24.2 us  [expand(): call(expand_kernel, (steps,), [pl.BlockSpec((1, length, width), lambda i:...]
    ppermute x3 -> x0, starting transfers between devices: 4.07 us -> none  [total_small(): value = value + lax.ppermute(value, ('asset', 'sample'), pairs)]
    unnamed x4 -> x6, local copies, waits for them, and re-layouts: 2.68 us -> 0.02 us
    pallas_call x3 -> x5, Pallas kernels: 22.5 us -> 24.2 us  [project(): call(project_kernel, (steps,), [pl.BlockSpec((1, length, width), lambda i...]
  transfers between devices with their start and end apart: 31 -> 34, of which waited for: 19 -> 20; matrix products, arithmetic and copies ran while one was open for 1% -> 1% of each run, Pallas kernels for 37% -> 41%
where the time goes in v2:
time: 255 us; the launch traced here: 250 us
  Pallas kernels  160 us (63%)
  starting transfers between devices  51 us (20%)
  waiting for transfers between devices  34.6 us (14%)
    ppermute x30, starting transfers between devices, start(): self.arriving = lax.ppermute(self.sent, ('asset', 'sample'), pairs)  50.8 us
    pallas_call x1, Pallas kernels, final_iterations(): pl.pallas_call(functools.partial(final_kernel, width_all), out_shape=(out...  36.6 us
    pallas_call x8, Pallas kernels, apply(): call(apply_kernel, (steps,), [pl.BlockSpec((1, length, width), lambda i:...  35.4 us
    ppermute x30, waiting for transfers between devices, start(): self.arriving = lax.ppermute(self.sent, ('asset', 'sample'), pairs)  33 us
    pallas_call x5, Pallas kernels, project(): call(project_kernel, (steps,), [pl.BlockSpec((1, length, width), lambda i...  24.2 us
    pallas_call x3, Pallas kernels, expand(): call(expand_kernel, (steps,), [pl.BlockSpec((1, length, width), lambda i:...  24.2 us
    pallas_call x2, Pallas kernels, partial_grams(): call(body, (rows // height,), [pl.BlockSpec((height, size), lambda i: (i,...  19.3 us
    pallas_call x2, Pallas kernels, normalise(): pl.pallas_call(functools.partial(normal_kernel, width_all), in_specs=[who...  10.6 us
  transfers between devices with their start and end apart: 34, of which 20 were waited for; matrix products, arithmetic and copies ran while one was open for 1% of the time, Pallas kernels for 41%

profile of v2, /device:TPU:0, one launch (start us, length us, event | category | flops | bytes accessed | tf_op | source)
XLA Modules:
  0.0 250.5 jit_solution(1637865405265504544)
XLA Ops:
  0.7 10.8 %shard_map.41 = f32[128,1024]{1,0:T(8,128)S(1)} custom-call(f32[2,1024,4096]{2,1,0:T(8,128)} %x_ref.31, f32[4096,128]{1,0:T(8,128)} %panel_ref.9, f32[8,128]{1,0:T(8,128)S(1)} %broadcast_in_dim.3.token_ref), custom_call_target="tpu_custom_call" | custom-call | flops 4294967296 | bytes 16777216 | tf_op jit(solution)/shard_map/pallas_call | solution.py:175
  21.1 3.3 %shard_map.43 = f32[128,1024]{1,0:T(8,128)S(1)} custom-call(f32[2,1024,4096]{2,1,0:T(8,128)} %x_ref.31, f32[4096,128]{1,0:T(8,128)} %panel_ref.9, f32[32,1024]{1,0:T(8,128)S(1)} %dynamic-slice_bitcast_fusion.7.token_ref), custom_call_target="tpu_custom_call" | custom-call | flops 1073741824 | bytes 4194304 | tf_op jit(solution)/shard_map/pallas_call | solution.py:175
  27.6 3.3 %shard_map.44 = f32[128,1024]{1,0:T(8,128)S(1)} custom-call(f32[2,1024,4096]{2,1,0:T(8,128)} %x_ref.31, f32[4096,128]{1,0:T(8,128)} %panel_ref.9, f32[16,1024]{1,0:T(8,128)S(1)} %dynamic-slice_bitcast_fusion.11.token_ref), custom_call_target="tpu_custom_call" | custom-call | flops 1073741824 | bytes 4194304 | tf_op jit(solution)/shard_map/pallas_call | solution.py:175
  53.1 4.4 %shard_map.46 = f32[1024,128]{1,0:T(8,128)S(1)} custom-call(f32[2,1024,4096]{2,1,0:T(8,128)} %x_ref.31, f32[128,1024]{1,0:T(8,128)S(1)} %maximum_select_fusion.scores_ref.first_ref, f32[16,1024]{1,0:T(8,128)S(1)} %dynamic-slice_bitcast_fusion.10.token_ref), custom_call_target="tpu_custom_call" | custom-call | flops 2147483648 | bytes 4194304 | tf_op jit(solution)/shard_map/pallas_call | solution.py:233
  58.9 4.4 %shard_map.47 = f32[1024,128]{1,0:T(8,128)S(1)} custom-call(f32[2,1024,4096]{2,1,0:T(8,128)} %x_ref.31, f32[128,1024]{1,0:T(8,128)S(1)} %maximum_select_fusion.scores_ref.first_ref, f32[16,1024]{1,0:T(8,128)S(1)} %bitcast_add_fusion.10.token_ref), custom_call_target="tpu_custom_call" | custom-call | flops 2147483648 | bytes 4194304 | tf_op jit(solution)/shard_map/pallas_call | solution.py:233
  63.7 4.4 %shard_map.48 = f32[1024,128]{1,0:T(8,128)S(1)} custom-call(f32[2,1024,4096]{2,1,0:T(8,128)} %x_ref.31, f32[128,1024]{1,0:T(8,128)S(1)} %maximum_select_fusion.scores_ref.first_ref, f32[32,1024]{1,0:T(8,128)S(1)} %maximum_select_fusion.11.token_ref), custom_call_target="tpu_custom_call" | custom-call | flops 2147483648 | bytes 4194304 | tf_op jit(solution)/shard_map/pallas_call | solution.py:233
  68.5 4.7 %collective-permute-start.11 = (f32[64,1024]{1,0:T(8,128)S(1)}, f32[64,1024]{1,0:T(8,128)S(1)}, u32[]{:S(2)}, u32[]{:S(2)}) collective-permute-start(f32[64,1024]{1,0:T(8,128)S(1)} %maximum_select_fusion.7.token_ref), channel_id=1, source_target_pairs={{0,2},{1,5},{2,0},{3,7},{4,6},{5,1},{6,4},{7,3},{8,10},{9,13},{10,... | collective-permute-start | bytes 786440 | tf_op jit(solution)/shard_map/ppermute | solution.py:520
  73.3 4.4 %shard_map.49 = f32[1024,128]{1,0:T(8,128)S(1)} custom-call(f32[2,1024,4096]{2,1,0:T(8,128)} %x_ref.31, f32[128,1024]{1,0:T(8,128)S(1)} %maximum_select_fusion.scores_ref.first_ref, f32[64,1024]{1,0:T(8,128)S(1)} %maximum_select_fusion.7.token_ref), custom_call_target="tpu_custom_call" | custom-call | flops 2147483648 | bytes 4194304 | tf_op jit(solution)/shard_map/pallas_call | solution.py:233
  79.9 4.7 %shard_map.50 = f32[1024,128]{1,0:T(8,128)S(1)} custom-call(f32[2,1024,4096]{2,1,0:T(8,128)} %x_ref.31, f32[128,1024]{1,0:T(8,128)S(1)} %maximum_select_fusion.1.scores_ref.first_ref, f32[512,128]{1,0:T(8,128)S(1)} %dynamic-slice_bitcast_fusion.1.token_ref), custom_call_target="tpu_custom_call" | custom-call | flops 2147483648 | bytes 4194304 | tf_op jit(solution)/shard_map/pallas_call | solution.py:233
  84.8 4.4 %shard_map.51 = f32[1024,128]{1,0:T(8,128)S(1)} custom-call(f32[2,1024,4096]{2,1,0:T(8,128)} %x_ref.31, f32[128,1024]{1,0:T(8,128)S(1)} %maximum_select_fusion.1.scores_ref.first_ref, f32[256,128]{1,0:T(8,128)S(1)} %dynamic-slice_bitcast_fusion.5.token_ref), custom_call_target="tpu_custom_call" | custom-call | flops 2147483648 | bytes 4194304 | tf_op jit(solution)/shard_map/pallas_call | solution.py:233
  89.8 4.4 %shard_map.52 = f32[1024,128]{1,0:T(8,128)S(1)} custom-call(f32[2,1024,4096]{2,1,0:T(8,128)} %x_ref.31, f32[128,1024]{1,0:T(8,128)S(1)} %maximum_select_fusion.1.scores_ref.first_ref, f32[128,128]{1,0:T(8,128)S(1)} %dynamic-slice_bitcast_fusion.9.token_ref), custom_call_target="tpu_custom_call" | custom-call | flops 2147483648 | bytes 4194304 | tf_op jit(solution)/shard_map/pallas_call | solution.py:233
  97.2 4.4 %shard_map.53 = f32[1024,128]{1,0:T(8,128)S(1)} custom-call(f32[2,1024,4096]{2,1,0:T(8,128)} %x_ref.31, f32[128,1024]{1,0:T(8,128)S(1)} %maximum_select_fusion.1.scores_ref.first_ref, f32[128,128]{1,0:T(8,128)S(1)} %bitcast_add_fusion.9.token_ref), custom_call_target="tpu_custom_call" | custom-call | flops 2147483648 | bytes 4194304 | tf_op jit(solution)/shard_map/pallas_call | solution.py:233
  117.2 5.3 %shard_map.54.scores_ref = f32[128,1024]{1,0:T(8,128)S(1)} custom-call(f32[128,1024]{1,0:T(8,128)S(1)} %maximum_select_fusion.scores_ref.first_ref, f32[1024,128]{1,0:T(8,128)S(1)} %maximum_select_fusion.2.second_ref, f32[128,128]{1,0:T(8,128)S(1)} %dynamic-slice_bitcast_fusion.8.token_ref), custom_call_target="tpu_custom_call" | custom-call | flops 6000000000 | bytes 1572864 | tf_op jit(solution)/shard_map/pallas_call | solution.py:300
  124.4 6.3 %shard_map.55.rest_0_ = f32[4096,128]{1,0:T(8,128)} custom-call(f32[2,1024,4096]{2,1,0:T(8,128)} %x_ref.31, f32[128,1024]{1,0:T(8,128)S(1)} %shard_map.54.scores_ref, f32[128,128]{1,0:T(8,128)S(1)} %bitcast_add_fusion.8.token_ref), custom_call_target="tpu_custom_call" | custom-call | flops 2147483648 | bytes 8388608 | tf_op jit(solution)/shard_map/pallas_call | solution.py:273
  131.9 6.4 %shard_map.56.own0 = f32[4096,128]{1,0:T(8,128)} custom-call(f32[2,1024,4096]{2,1,0:T(8,128)} %x_ref.31, f32[128,1024]{1,0:T(8,128)S(1)} %shard_map.54.scores_ref, f32[256,128]{1,0:T(8,128)S(1)} %maximum_select_fusion.13.token_ref, f32[4096,128]{1,0:T(8,128)} %shard_map.55.rest_0_), custom_call_target="tpu_custom_call", output_to_operand_aliasing={{}: (3, {})} | custom-call | flops 2147483648 | bytes 8388608 | tf_op jit(solution)/shard_map/pallas_call | solution.py:273
  139.8 4.9 %collective-permute-done.23 = f32[512,128]{1,0:T(8,128)S(1)} collective-permute-done((f32[512,128]{1,0:T(8,128)S(1)}, f32[512,128]{1,0:T(8,128)S(1)}, u32[]{:S(2)}, u32[]{:S(2)}) %collective-permute-start.23) | collective-permute-done | bytes 262176 | tf_op jit(solution)/shard_map/ppermute | solution.py:520
  144.8 5.3 %shard_map.57.scores_ref = f32[128,1024]{1,0:T(8,128)S(1)} custom-call(f32[128,1024]{1,0:T(8,128)S(1)} %maximum_select_fusion.1.scores_ref.first_ref, f32[1024,128]{1,0:T(8,128)S(1)} %maximum_select_fusion.3.second_ref, f32[8,128]{1,0:T(8,128)S(1)} %copy-done.1), custom_call_target="tpu_custom_call" | custom-call | flops 6000000000 | bytes 1572864 | tf_op jit(solution)/shard_map/pallas_call | solution.py:300
  150.1 11.5 %shard_map.58.own1 = f32[4096,128]{1,0:T(8,128)} custom-call(f32[2,1024,4096]{2,1,0:T(8,128)} %x_ref.31, f32[128,1024]{1,0:T(8,128)S(1)} %shard_map.57.scores_ref, f32[8,128]{1,0:T(8,128)S(1)} %copy-done.1), custom_call_target="tpu_custom_call" | custom-call | flops 4294967296 | bytes 16777216 | tf_op jit(solution)/shard_map/pallas_call | solution.py:273
  161.6 5.0 %shard_map.59 = f32[3,128,128]{2,1,0:T(8,128)} custom-call(f32[4096,128]{1,0:T(8,128)} %shard_map.56.own0, f32[4096,128]{1,0:T(8,128)} %shard_map.58.own1), custom_call_target="tpu_custom_call" | custom-call | flops 4026531840 | bytes 4194304 | tf_op jit(solution)/shard_map/pallas_call | solution.py:354
  168.1 14.3 %shard_map.60 = f32[2,128,128]{2,1,0:T(8,128)} custom-call(f32[4096,128]{1,0:T(8,128)} %shard_map.56.own0, f32[4096,128]{1,0:T(8,128)} %shard_map.58.own1, f32[4096,128]{1,0:T(8,128)} %collective-permute-done.24.other0, f32[4096,128]{1,0:T(8,128)} %collective-permute-done.25.other1), custom_call_target="tpu_custom_call" | custom-call | flops 4026531840 | bytes 8388608 | tf_op jit(solution)/shard_map/pallas_call | solution.py:354
  184.0 3.6 %collective-permute-done.29 = f32[2,128,128]{2,1,0:T(8,128)S(1)} collective-permute-done((f32[2,128,128]{2,1,0:T(8,128)}, f32[2,128,128]{2,1,0:T(8,128)S(1)}, u32[]{:S(2)}, u32[]{:S(2)}) %collective-permute-start.29) | collective-permute-done | bytes 131104 | tf_op jit(solution)/shard_map/ppermute | solution.py:557
  196.5 5.5 %collective-permute-done.31 = f32[2,128,128]{2,1,0:T(8,128)S(1)} collective-permute-done((f32[2,128,128]{2,1,0:T(8,128)S(1)}, f32[2,128,128]{2,1,0:T(8,128)S(1)}, u32[]{:S(2)}, u32[]{:S(2)}) %collective-permute-start.31) | collective-permute-done | bytes 131104 | tf_op jit(solution)/shard_map/ppermute | solution.py:557
  203.8 36.6 %shard_map.61 = (f32[4,128,128]{2,1,0:T(8,128)S(1)}, f32[4,128,128]{2,1,0:T(8,128)S(1)}) custom-call(f32[5,128,128]{2,1,0:T(8,128)S(1)} %get-tuple-element.71.first, f32[5,128,128]{2,1,0:T(8,128)S(1)} %get-tuple-element.70.second, f32[2,128,128]{2,1,0:T(8,128)S(1)} %get-tuple-element.73.start0, f32[2,128,128]{2,1,0:T(8,128)S(1)} %get-tuple-element.72.start1), custom_call_target="tpu_custom_call" | custom-call | tf_op jit(solution)/shard_map/pallas_call | solution.py:415
  240.4 9.8 %shard_map.62 = (f32[2,4096,128]{2,1,0:T(8,128)}, f32[4096,128]{1,0:T(8,128)}) custom-call(f32[4096,128]{1,0:T(8,128)} %shard_map.56.own0, f32[4096,128]{1,0:T(8,128)} %shard_map.58.own1, f32[4096,128]{1,0:T(8,128)} %collective-permute-done.24.other0, f32[4096,128]{1,0:T(8,128)} %collective-permute-done.25.other1, ...), custom_call_target="tpu_custom_call" | custom-call | flops 3221225472 | bytes 14680064 | tf_op jit(solution)/shard_map/pallas_call | solution.py:466
  (124 shorter events, 76.9 us)
Async XLA Ops:
  11.6 7.4 %collective-permute-start = (f32[64,1024]{1,0:T(8,128)S(1)}, f32[64,1024]{1,0:T(8,128)S(1)}, u32[]{:S(2)}, u32[]{:S(2)}) collective-permute-start(f32[64,1024]{1,0:T(8,128)S(1)} %dynamic-slice_bitcast_fusion.3.token_ref), channel_id=1, source_target_pairs={{0,2},{1,5},{2,0},{3,7},{4,6},{5,1},{6,4},{7,3},{8,10},{9,13},{10,... | collective-permute-start | bytes 786440 | tf_op jit(solution)/shard_map/ppermute | solution.py:520
  24.6 6.4 %collective-permute-start.2 = (f32[16,1024]{1,0:T(8,128)S(1)}, f32[16,1024]{1,0:T(8,128)S(1)}, u32[]{:S(2)}, u32[]{:S(2)}) collective-permute-start(f32[16,1024]{1,0:T(8,128)S(1)} %dynamic-slice_bitcast_fusion.11.token_ref), channel_id=1, source_target_pairs={{0,8},{1,3},{2,10},{3,1},{4,12},{5,7},{6,14},{7,5},{8,0},{9,11},{1... | collective-permute-start | bytes 196616 | tf_op jit(solution)/shard_map/ppermute | solution.py:520
  36.4 6.4 %collective-permute-start.6 = (f32[64,1024]{1,0:T(8,128)S(1)}, f32[64,1024]{1,0:T(8,128)S(1)}, u32[]{:S(2)}, u32[]{:S(2)}) collective-permute-start(f32[64,1024]{1,0:T(8,128)S(1)} %dynamic-slice_bitcast_fusion.2), channel_id=1, source_target_pairs={{0,2},{1,5},{2,0},{3,7},{4,6},{5,1},{6,4},{7,3},{8,10},{9,13},{10,... | collective-permute-start | bytes 786440 | tf_op jit(solution)/shard_map/ppermute | solution.py:520
  38.0 7.8 %collective-permute-start.4 = (f32[32,1024]{1,0:T(8,128)S(1)}, f32[32,1024]{1,0:T(8,128)S(1)}, u32[]{:S(2)}, u32[]{:S(2)}) collective-permute-start(f32[32,1024]{1,0:T(8,128)S(1)} %maximum_select_fusion.10), channel_id=1, source_target_pairs={{0,4},{1,9},{2,6},{3,11},{4,0},{5,13},{6,2},{7,15},{8,12},{9,1},{1... | collective-permute-start | bytes 393224 | tf_op jit(solution)/shard_map/ppermute | solution.py:520
  42.9 7.1 %collective-permute-start.7 = (f32[32,1024]{1,0:T(8,128)S(1)}, f32[32,1024]{1,0:T(8,128)S(1)}, u32[]{:S(2)}, u32[]{:S(2)}) collective-permute-start(f32[32,1024]{1,0:T(8,128)S(1)} %dynamic-slice_bitcast_fusion.6), channel_id=1, source_target_pairs={{0,4},{1,9},{2,6},{3,11},{4,0},{5,13},{6,2},{7,15},{8,12},{9,1},{1... | collective-permute-start | bytes 393224 | tf_op jit(solution)/shard_map/ppermute | solution.py:520
  45.9 7.1 %collective-permute-start.5 = (f32[64,1024]{1,0:T(8,128)S(1)}, f32[64,1024]{1,0:T(8,128)S(1)}, u32[]{:S(2)}, u32[]{:S(2)}) collective-permute-start(f32[64,1024]{1,0:T(8,128)S(1)} %maximum_select_fusion.6), channel_id=1, source_target_pairs={{0,2},{1,5},{2,0},{3,7},{4,6},{5,1},{6,4},{7,3},{8,10},{9,13},{10,... | collective-permute-start | bytes 786440 | tf_op jit(solution)/shard_map/ppermute | solution.py:520
  50.1 7.4 %collective-permute-start.8 = (f32[16,1024]{1,0:T(8,128)S(1)}, f32[16,1024]{1,0:T(8,128)S(1)}, u32[]{:S(2)}, u32[]{:S(2)}) collective-permute-start(f32[16,1024]{1,0:T(8,128)S(1)} %dynamic-slice_bitcast_fusion.10.token_ref), channel_id=1, source_target_pairs={{0,8},{1,3},{2,10},{3,1},{4,12},{5,7},{6,14},{7,5},{8,0},{9,11},{1... | collective-permute-start | bytes 196616 | tf_op jit(solution)/shard_map/ppermute | solution.py:520
  57.5 5.9 %collective-permute-start.9 = (f32[16,1024]{1,0:T(8,128)S(1)}, f32[16,1024]{1,0:T(8,128)S(1)}, u32[]{:S(2)}, u32[]{:S(2)}) collective-permute-start(f32[16,1024]{1,0:T(8,128)S(1)} %bitcast_add_fusion.10.token_ref), channel_id=1, source_target_pairs={{0,8},{1,3},{2,10},{3,1},{4,12},{5,7},{6,14},{7,5},{8,0},{9,11},{1... | collective-permute-start | bytes 196616 | tf_op jit(solution)/shard_map/ppermute | solution.py:520
  68.5 9.1 %collective-permute-start.11 = (f32[64,1024]{1,0:T(8,128)S(1)}, f32[64,1024]{1,0:T(8,128)S(1)}, u32[]{:S(2)}, u32[]{:S(2)}) collective-permute-start(f32[64,1024]{1,0:T(8,128)S(1)} %maximum_select_fusion.7.token_ref), channel_id=1, source_target_pairs={{0,2},{1,5},{2,0},{3,7},{4,6},{5,1},{6,4},{7,3},{8,10},{9,13},{10,... | collective-permute-start | bytes 786440 | tf_op jit(solution)/shard_map/ppermute | solution.py:520
  77.8 6.7 %collective-permute-start.12 = (f32[512,128]{1,0:T(8,128)S(1)}, f32[512,128]{1,0:T(8,128)S(1)}, u32[]{:S(2)}, u32[]{:S(2)}) collective-permute-start(f32[512,128]{1,0:T(8,128)S(1)} %dynamic-slice_bitcast_fusion.1.token_ref), channel_id=1, source_target_pairs={{0,2},{1,5},{2,0},{3,7},{4,6},{5,1},{6,4},{7,3},{8,10},{9,13},{10,... | collective-permute-start | bytes 786440 | tf_op jit(solution)/shard_map/ppermute | solution.py:520
  94.9 6.6 %collective-permute-start.15 = (f32[128,128]{1,0:T(8,128)S(1)}, f32[128,128]{1,0:T(8,128)S(1)}, u32[]{:S(2)}, u32[]{:S(2)}) collective-permute-start(f32[128,128]{1,0:T(8,128)S(1)} %bitcast_add_fusion.9.token_ref), channel_id=1, source_target_pairs={{0,8},{1,3},{2,10},{3,1},{4,12},{5,7},{6,14},{7,5},{8,0},{9,11},{1... | collective-permute-start | bytes 196616 | tf_op jit(solution)/shard_map/ppermute | solution.py:520
  101.7 6.4 %collective-permute-start.18 = (f32[512,128]{1,0:T(8,128)S(1)}, f32[512,128]{1,0:T(8,128)S(1)}, u32[]{:S(2)}, u32[]{:S(2)}) collective-permute-start(f32[512,128]{1,0:T(8,128)S(1)} %dynamic-slice_bitcast_fusion), channel_id=1, source_target_pairs={{0,2},{1,5},{2,0},{3,7},{4,6},{5,1},{6,4},{7,3},{8,10},{9,13},{10,... | collective-permute-start | bytes 786440 | tf_op jit(solution)/shard_map/ppermute | solution.py:520
  103.4 7.3 %collective-permute-start.16 = (f32[256,128]{1,0:T(8,128)S(1)}, f32[256,128]{1,0:T(8,128)S(1)}, u32[]{:S(2)}, u32[]{:S(2)}) collective-permute-start(f32[256,128]{1,0:T(8,128)S(1)} %maximum_select_fusion.12), channel_id=1, source_target_pairs={{0,4},{1,9},{2,6},{3,11},{4,0},{5,13},{6,2},{7,15},{8,12},{9,1},{1... | collective-permute-start | bytes 393224 | tf_op jit(solution)/shard_map/ppermute | solution.py:520
  110.8 6.4 %collective-permute-start.17 = (f32[512,128]{1,0:T(8,128)S(1)}, f32[512,128]{1,0:T(8,128)S(1)}, u32[]{:S(2)}, u32[]{:S(2)}) collective-permute-start(f32[512,128]{1,0:T(8,128)S(1)} %maximum_select_fusion.8), channel_id=1, source_target_pairs={{0,2},{1,5},{2,0},{3,7},{4,6},{5,1},{6,4},{7,3},{8,10},{9,13},{10,... | collective-permute-start | bytes 786440 | tf_op jit(solution)/shard_map/ppermute | solution.py:520
  113.3 9.2 %collective-permute-start.20 = (f32[128,128]{1,0:T(8,128)S(1)}, f32[128,128]{1,0:T(8,128)S(1)}, u32[]{:S(2)}, u32[]{:S(2)}) collective-permute-start(f32[128,128]{1,0:T(8,128)S(1)} %dynamic-slice_bitcast_fusion.8.token_ref), channel_id=1, source_target_pairs={{0,8},{1,3},{2,10},{3,1},{4,12},{5,7},{6,14},{7,5},{8,0},{9,11},{1... | collective-permute-start | bytes 196616 | tf_op jit(solution)/shard_map/ppermute | solution.py:520
  122.6 8.2 %collective-permute-start.21 = (f32[128,128]{1,0:T(8,128)S(1)}, f32[128,128]{1,0:T(8,128)S(1)}, u32[]{:S(2)}, u32[]{:S(2)}) collective-permute-start(f32[128,128]{1,0:T(8,128)S(1)} %bitcast_add_fusion.8.token_ref), channel_id=1, source_target_pairs={{0,8},{1,3},{2,10},{3,1},{4,12},{5,7},{6,14},{7,5},{8,0},{9,11},{1... | collective-permute-start | bytes 196616 | tf_op jit(solution)/shard_map/ppermute | solution.py:520
  130.8 7.5 %collective-permute-start.22 = (f32[256,128]{1,0:T(8,128)S(1)}, f32[256,128]{1,0:T(8,128)S(1)}, u32[]{:S(2)}, u32[]{:S(2)}) collective-permute-start(f32[256,128]{1,0:T(8,128)S(1)} %maximum_select_fusion.13.token_ref), channel_id=1, source_target_pairs={{0,4},{1,9},{2,6},{3,11},{4,0},{5,13},{6,2},{7,15},{8,12},{9,1},{1... | collective-permute-start | bytes 393224 | tf_op jit(solution)/shard_map/ppermute | solution.py:520
  138.3 6.4 %collective-permute-start.23 = (f32[512,128]{1,0:T(8,128)S(1)}, f32[512,128]{1,0:T(8,128)S(1)}, u32[]{:S(2)}, u32[]{:S(2)}) collective-permute-start(f32[512,128]{1,0:T(8,128)S(1)} %maximum_select_fusion.9), channel_id=1, source_target_pairs={{0,2},{1,5},{2,0},{3,7},{4,6},{5,1},{6,4},{7,3},{8,10},{9,13},{10,... | collective-permute-start | bytes 786440 | tf_op jit(solution)/shard_map/ppermute | solution.py:520
  139.8 28.2 %collective-permute-start.24 = (f32[4096,128]{1,0:T(8,128)}, f32[4096,128]{1,0:T(8,128)}, u32[]{:S(2)}, u32[]{:S(2)}) collective-permute-start(f32[4096,128]{1,0:T(8,128)} %shard_map.56.own0), channel_id=1, source_target_pairs={{0,1},{1,0},{2,3},{3,2},{4,5},{5,4},{6,7},{7,6},{8,9},{9,8},{10,11... | collective-permute-start | bytes 6291464 | tf_op jit(solution)/shard_map/ppermute | solution.py:570
  161.6 6.5 %collective-permute-start.25 = (f32[4096,128]{1,0:T(8,128)}, f32[4096,128]{1,0:T(8,128)}, u32[]{:S(2)}, u32[]{:S(2)}) collective-permute-start(f32[4096,128]{1,0:T(8,128)} %shard_map.58.own1), channel_id=1, source_target_pairs={{0,1},{1,0},{2,3},{3,2},{4,5},{5,4},{6,7},{7,6},{8,9},{9,8},{10,11... | collective-permute-start | bytes 6291464 | tf_op jit(solution)/shard_map/ppermute | solution.py:570
  166.6 15.7 %collective-permute-start.26 = (f32[3,128,128]{2,1,0:T(8,128)}, f32[3,128,128]{2,1,0:T(8,128)S(1)}, u32[]{:S(2)}, u32[]{:S(2)}) collective-permute-start(f32[3,128,128]{2,1,0:T(8,128)} %shard_map.59), channel_id=1, source_target_pairs={{0,2},{1,5},{2,0},{3,7},{4,6},{5,1},{6,4},{7,3},{8,10},{9,13},{10,... | collective-permute-start | bytes 589832 | tf_op jit(solution)/shard_map/ppermute | solution.py:557
  183.0 7.4 %collective-permute-start.27 = (f32[3,128,128]{2,1,0:T(8,128)S(1)}, f32[3,128,128]{2,1,0:T(8,128)S(1)}, u32[]{:S(2)}, u32[]{:S(2)}) collective-permute-start(f32[3,128,128]{2,1,0:T(8,128)S(1)} %add.181), channel_id=1, source_target_pairs={{0,4},{1,9},{2,6},{3,11},{4,0},{5,13},{6,2},{7,15},{8,12},{9,1},{1... | collective-permute-start | bytes 589832 | tf_op jit(solution)/shard_map/ppermute | solution.py:557
  190.4 11.6 %collective-permute-start.28 = (f32[3,128,128]{2,1,0:T(8,128)S(1)}, f32[3,128,128]{2,1,0:T(8,128)S(1)}, u32[]{:S(2)}, u32[]{:S(2)}) collective-permute-start(f32[3,128,128]{2,1,0:T(8,128)S(1)} %add.182), channel_id=1, source_target_pairs={{0,8},{1,3},{2,10},{3,1},{4,12},{5,7},{6,14},{7,5},{8,0},{9,11},{1... | collective-permute-start | bytes 589832 | tf_op jit(solution)/shard_map/ppermute | solution.py:557
  194.0 8.0 %collective-permute-start.31 = (f32[2,128,128]{2,1,0:T(8,128)S(1)}, f32[2,128,128]{2,1,0:T(8,128)S(1)}, u32[]{:S(2)}, u32[]{:S(2)}) collective-permute-start(f32[2,128,128]{2,1,0:T(8,128)S(1)} %add.185), channel_id=1, source_target_pairs={{0,8},{1,3},{2,10},{3,1},{4,12},{5,7},{6,14},{7,5},{8,0},{9,11},{1... | collective-permute-start | bytes 393224 | tf_op jit(solution)/shard_map/ppermute | solution.py:557
  (13 other events, 90.6 us)
